TPU v7x, 512 devices: a whole 4x4x16 slice. The times are simulated.
512 devices in a mesh: seq: 64 (over y, z), dp: 8 (over x, core).
Axes of the slice: x: 4, y: 4, z: 16, core: 2. Of those that a mesh axis runs over, the one named last changes fastest.
Arguments:
- queries: bfloat16 [8, 512, 4096], P('dp', 'seq'), may hold values from -8 to 8
- key_vectors: bfloat16 [8, 8192, 4096], P('dp', 'seq'), may hold values from -6 to 6
- value_vectors: bfloat16 [8, 8192, 4096], P('dp', 'seq'), may hold values from -6 to 6
- saved_out: bfloat16 [8, 512, 4096], P('dp', 'seq'), may hold values from -6 to 6
- grad_out: bfloat16 [8, 512, 4096], P('dp', 'seq'), may hold values from -192 to 192
- out_weight: bfloat16 [4096, 4096], P('seq', 'dp'), may hold values from -0.09375 to 0.09375
- window_start: int32 [8], P('dp'), may hold values from 1 to 7680
- block_order: int32 [64], replicated, may hold values from 0 to 63, each once
Outputs:
- grad_queries: bfloat16 [8, 512, 4096], P('dp', 'seq')
- grad_keys: bfloat16 [8, 8192, 4096], P('dp', 'seq')
- grad_values: bfloat16 [8, 8192, 4096], P('dp', 'seq')
- grad_weight: float32 [4096, 4096], P('seq', 'dp')
Inputs may be any that keep to these rules, and one draw needn't show every extreme that they name: `block_order`: a permutation of the 64 query blocks. `window_start`: the window's last query lies inside the prefix.
All inputs are finite; a program needn't handle non-finite values.
Results may differ from a plain program's by a relative error of at most 0.017.
Values may be sent and summed in bfloat16 or wider, within the bound.
A program may use at most 64 MiB of HBM per device.

v0:
```python
import math

import jax
import jax.numpy as jnp
from jax import lax
from jax.sharding import PartitionSpec as P

H = 32
HD = 128


masked_low = -1e30


def from_partner(value, axis, bit):
    return lax.ppermute(value, axis, [(i, i ^ 1 << bit) for i in range(lax.axis_size(axis))])


def on_device(
    queries, key_vectors, value_vectors, saved_out, grad_out, out_weight, window_start, block_order
):
    n_seq = lax.axis_size("seq")
    n_data = lax.axis_size("dp")
    part_count = max(1, n_seq // H)
    per_dev = max(1, H // n_seq)
    groups = n_seq // part_count
    head_cols = per_dev * HD
    col_share = head_cols // part_count
    member = lax.axis_index("seq") % part_count
    q_rows = queries.shape[1]
    k_rows = key_vectors.shape[1]
    k_part = k_rows // part_count
    window = q_rows * n_seq
    n_keys = n_seq * k_part
    inv_root = 1.0 / math.sqrt(HD)

    def spread_rows(array):
        placed = array.reshape(q_rows, groups, 1, head_cols).transpose(1, 2, 0, 3)
        return jnp.broadcast_to(placed, (groups, part_count, q_rows, head_cols)).reshape(
            n_seq * q_rows, head_cols
        )

    def split_keys(array):
        placed = array.reshape(part_count, k_part, groups, head_cols).transpose(2, 0, 1, 3)
        return placed.reshape(n_keys, head_cols)

    query_rows, out_rows, key_rows, value_rows = (
        lax.all_to_all(spread_rows(queries[0]), "seq", split_axis=0, concat_axis=0, tiled=True),
        lax.all_to_all(spread_rows(saved_out[0]), "seq", split_axis=0, concat_axis=0, tiled=True),
        lax.all_to_all(split_keys(key_vectors[0]), "seq", split_axis=0, concat_axis=0, tiled=True),
        lax.all_to_all(
            split_keys(value_vectors[0]), "seq", split_axis=0, concat_axis=0, tiled=True
        ),
    )
    row_block = lax.all_gather(out_weight, "dp", axis=1, tiled=True)
    partner = from_partner(row_block, "seq", 0)
    head_rows = jnp.where(
        member == 0,
        jnp.concatenate([row_block, partner], 0),
        jnp.concatenate([partner, row_block], 0),
    )
    contract_cols = (((1,), (1,)), ((), ()))
    contract_rows = (((0,), (0,)), ((), ()))
    grad_rows = grad_out[0]
    all_grad = lax.all_gather(grad_rows, "seq", axis=0, tiled=True)
    context = lax.dot_general(
        all_grad, head_rows, contract_cols, preferred_element_type=jnp.float32
    ).astype(jnp.bfloat16)
    own_out = lax.dynamic_slice_in_dim(out_rows, member * col_share, col_share, 1)
    weight_grad = lax.psum_scatter(
        lax.dot_general(
            all_grad, own_out, contract_rows, preferred_element_type=jnp.float32
        ).astype(jnp.bfloat16),
        "dp",
        scatter_dimension=0,
        tiled=True,
    ).astype(jnp.float32)
    grad_weight = weight_grad.T / (n_data * window)
    first_pos = window_start[0]
    query_pos = (
        first_pos + (block_order[:, None] * q_rows + jnp.arange(q_rows, dtype=jnp.int32)[None, :])
    ).reshape(window)
    key_pos = (
        (jnp.arange(n_seq, dtype=jnp.int32) * k_rows)[:, None]
        + member * k_part
        + jnp.arange(k_part, dtype=jnp.int32)[None, :]
    ).reshape(n_keys)
    query_heads = query_rows.reshape(window, per_dev, HD)
    key_heads = key_rows.reshape(n_keys, per_dev, HD)
    value_heads = value_rows.reshape(n_keys, per_dev, HD)
    context_heads = context.reshape(window, per_dev, HD)
    row_delta = jnp.sum(
        (context.astype(jnp.float32) * out_rows.astype(jnp.float32)).reshape(window, per_dev, HD),
        -1,
    ).T
    block_len = min(512, n_keys)
    loop_end = n_keys // block_len

    def block_scores(number):
        key_block = lax.dynamic_slice_in_dim(key_heads, number * block_len, block_len, 0)
        pos_block = lax.dynamic_slice_in_dim(key_pos, number * block_len, block_len, 0)
        raw = (
            jnp.einsum("qhd,khd->hqk", query_heads, key_block, preferred_element_type=jnp.float32)
            * inv_root
        )
        seen = pos_block[None, None, :] <= query_pos[None, :, None]
        return (key_block, seen, jnp.where(seen, raw, masked_low))

    def stats_step(number, carry):
        row_max, row_sum = carry
        key_block, seen, scores = block_scores(number)
        new_max = jnp.maximum(row_max, jnp.max(scores, 2))
        row_sum = row_sum * jnp.exp(row_max - new_max) + jnp.sum(
            jnp.where(seen, jnp.exp(scores - new_max[..., None]), 0.0), 2
        )
        return (new_max, row_sum)

    row_max, row_sum = lax.fori_loop(
        0,
        loop_end,
        stats_step,
        (
            jnp.full((per_dev, window), masked_low, jnp.float32),
            jnp.zeros((per_dev, window), jnp.float32),
        ),
    )
    far_max, far_sum = from_partner((row_max, row_sum), "seq", 0)
    joint_max = jnp.maximum(row_max, far_max)
    row_sum = row_sum * jnp.exp(row_max - joint_max) + far_sum * jnp.exp(far_max - joint_max)
    row_max = joint_max
    log_norm = row_max + jnp.log(row_sum)

    def grad_step(number, carry):
        query_grad, key_grads, value_grads = carry
        key_block, seen, scores = block_scores(number)
        value_block = lax.dynamic_slice_in_dim(value_heads, number * block_len, block_len, 0)
        attend = jnp.where(seen, jnp.exp(scores - log_norm[..., None]), 0.0)
        value_piece = jnp.einsum(
            "hqk,qhd->khd",
            attend.astype(jnp.bfloat16),
            context_heads,
            preferred_element_type=jnp.float32,
        ).astype(jnp.bfloat16)
        dprob = jnp.einsum(
            "qhd,khd->hqk", context_heads, value_block, preferred_element_type=jnp.float32
        )
        dscore = (attend * (dprob - row_delta[..., None])).astype(jnp.bfloat16)
        query_grad = query_grad + jnp.einsum(
            "hqk,khd->qhd", dscore, key_block, preferred_element_type=jnp.float32
        )
        key_piece = (
            jnp.einsum("hqk,qhd->khd", dscore, query_heads, preferred_element_type=jnp.float32)
            * inv_root
        ).astype(jnp.bfloat16)
        key_grads = lax.dynamic_update_slice_in_dim(key_grads, key_piece, number * block_len, 0)
        value_grads = lax.dynamic_update_slice_in_dim(
            value_grads, value_piece, number * block_len, 0
        )
        return (query_grad, key_grads, value_grads)

    start_carry = (
        jnp.zeros((window, per_dev, HD), jnp.float32),
        jnp.zeros((n_keys, per_dev, HD), jnp.bfloat16),
        jnp.zeros((n_keys, per_dev, HD), jnp.bfloat16),
    )
    query_grad, key_grads, value_grads = lax.fori_loop(0, loop_end, grad_step, start_carry)
    query_flat = query_grad.reshape(window, head_cols)
    kept_cols = lax.dynamic_slice_in_dim(query_flat, member * col_share, col_share, 1)
    sent_cols = lax.dynamic_slice_in_dim(query_flat, (1 - member) * col_share, col_share, 1)
    query_own = kept_cols + from_partner(sent_cols.astype(jnp.bfloat16), "seq", 0).astype(
        sent_cols.dtype
    )
    query_send = (query_own * inv_root).astype(jnp.bfloat16)
    query_back, key_back, value_back = (
        lax.all_to_all(query_send, "seq", split_axis=0, concat_axis=0, tiled=True),
        lax.all_to_all(
            key_grads.reshape(n_keys, head_cols), "seq", split_axis=0, concat_axis=0, tiled=True
        ),
        lax.all_to_all(
            value_grads.reshape(n_keys, head_cols), "seq", split_axis=0, concat_axis=0, tiled=True
        ),
    )
    grad_queries = (
        query_back.reshape(n_seq, q_rows, col_share)
        .transpose(1, 0, 2)
        .reshape(q_rows, n_seq * col_share)
    )

    def keys_home(array):
        return (
            array.reshape(groups, part_count, k_part, head_cols)
            .transpose(1, 2, 0, 3)
            .reshape(k_rows, groups * head_cols)
        )

    return (grad_queries[None], keys_home(key_back)[None], keys_home(value_back)[None], grad_weight)


def solution(mesh):
    return jax.shard_map(
        on_device,
        mesh=mesh,
        in_specs=(
            P("dp", "seq", None),
            P("dp", "seq", None),
            P("dp", "seq", None),
            P("dp", "seq", None),
            P("dp", "seq", None),
            P("seq", "dp"),
            P("dp"),
            P(),
        ),
        out_specs=(
            P("dp", "seq", None),
            P("dp", "seq", None),
            P("dp", "seq", None),
            P("seq", "dp"),
        ),
        check_vma=False,
    )
```

profile of v0, /device:TPU:24, one launch (start us, length us, event | category | flops | bytes accessed | tf_op | source)
XLA Modules:
  0.0 422.5 jit_solution(5170235938034907344)
XLA Ops:
  8.1 34.0 %all_to_all.66 = bf16[64,8,128]{2,1,0:T(8,128)(2,1)S(1)} all-to-all(bf16[64,8,128]{2,1,0:T(8,128)(2,1)S(1)} %bitcast.207), channel_id=1, replica_groups=mesh['seq'=64,'dp'=8] {'seq'}, dimensions={0} | all-to-all | bytes 262144 | tf_op jit(solution)/shard_map/all_to_all | solution.py:48
  42.2 1.5 broadcast_in_dim.66
  43.7 6.4 %all-to-all-start.3 = ((bf16[64,8,128]{2,1,0:T(8,128)(2,1)}), bf16[64,8,128]{2,1,0:T(8,128)(2,1)S(1)}, u32[]{:S(2)}, u32[]{:S(2)}) async-start(bf16[64,8,128]{2,1,0:T(8,128)(2,1)} %bitcast.18), calls=%async_computation.3 | async-start | bytes 262144 | tf_op jit(solution)/shard_map/all_to_all | solution.py:49
  50.1 1.4 copy.32
  51.5 1.4 copy.23
  52.9 12.3 %all-to-all-done.3 = bf16[64,8,128]{2,1,0:T(8,128)(2,1)S(1)} async-done(((bf16[64,8,128]{2,1,0:T(8,128)(2,1)}), bf16[64,8,128]{2,1,0:T(8,128)(2,1)S(1)}, u32[]{:S(2)}, u32[]{:S(2)}) %all-to-all-start.3) | async-done | bytes 131104 | tf_op jit(solution)/shard_map/all_to_all | solution.py:49
  65.2 6.5 %all-to-all-start = ((bf16[64,64,128]{2,1,0:T(8,128)(2,1)}), bf16[64,64,128]{2,1,0:T(8,128)(2,1)S(1)}, u32[]{:S(2)}, u32[]{:S(2)}) async-start(bf16[64,64,128]{2,1,0:T(8,128)(2,1)} %bitcast.1), calls=%async_computation | async-start | bytes 2097152 | tf_op jit(solution)/shard_map/all_to_all | solution.py:50
  72.4 14.6 %all_gather.6 = bf16[64,4096]{1,0:T(8,128)(2,1)} all-gather(bf16[64,512]{1,0:T(8,128)(2,1)S(1)} %copy-done.2), channel_id=1, replica_groups=mesh['seq'=64,'dp'=8] {'dp'}, dimensions={1}, use_global_device_ids=true | all-gather | bytes 589824 | tf_op jit(solution)/shard_map/all_gather | solution.py:55
  87.0 3.4 collective-permute-start.2
  90.8 1.4 copy.24
  92.2 36.2 %all-to-all-done = bf16[64,64,128]{2,1,0:T(8,128)(2,1)S(1)} async-done(((bf16[64,64,128]{2,1,0:T(8,128)(2,1)}), bf16[64,64,128]{2,1,0:T(8,128)(2,1)S(1)}, u32[]{:S(2)}, u32[]{:S(2)}) %all-to-all-start) | async-done | bytes 1048608 | tf_op jit(solution)/shard_map/all_to_all | solution.py:50
  128.5 6.4 %all-to-all-start.2 = ((bf16[64,64,128]{2,1,0:T(8,128)(2,1)}), bf16[64,64,128]{2,1,0:T(8,128)(2,1)S(1)}, u32[]{:S(2)}, u32[]{:S(2)}) async-start(bf16[64,64,128]{2,1,0:T(8,128)(2,1)} %bitcast.10), calls=%async_computation.2 | async-start | bytes 2097152 | tf_op jit(solution)/shard_map/all_to_all | solution.py:51
  134.9 12.2 %while.34 = (s32[]{:T(128)}, f32[1,512]{1,0:T(1,128)S(1)}, f32[1,512]{1,0:T(1,128)S(1)}, s32[4096]{0:T(1024)S(1)}, bf16[4096,1,128]{2,0,1:T(8,128)(2,1)S(1)}, /*...) while((s32[]{:T(128)}, f32[1,512]{1,0:T(1,128)S(1)}, ...), condition=%wide.region_3.4_spmd.clone, body=%wide.region_0.3_spmd.clone.sunk | while | flops 69209608 | bytes 2404802 | solution.py:118
  147.1 3.4 collective-permute-start.1
  150.5 2.5 collective-permute-start
  153.1 29.8 %collective-permute-done.1 = f32[1,512]{1,0:T(1,128)S(1)} collective-permute-done((f32[1,512]{1,0:T(1,128)S(1)}, f32[1,512]{1,0:T(1,128)S(1)}, u32[]{:S(2)}, u32[]{:S(2)}) %collective-permute-start.1) | collective-permute-done | bytes 2080 | tf_op jit(solution)/shard_map/ppermute | solution.py:16
  183.0 50.2 %all-gather.3.cloned.1.call-done = bf16[1,512,4096]{2,1,0:T(8,128)(2,1)} async-done(((bf16[1,8,4096]{2,1,0:T(8,128)(2,1)}), bf16[1,512,4096]{2,1,0:T(8,128)(2,1)}) %all-gather.3.cloned.1.call-update) | async-done | bytes 4194320 | tf_op jit(solution)/shard_map/all_gather | solution.py:65
  233.2 4.1 multiply_reduce_fusion
  238.6 40.4 %while.35 = (s32[]{:T(128)}, f32[512,1,128]{0,2,1:T(8,128)S(1)}, bf16[4096,1,128]{2,0,1:T(8,128)(2,1)S(1)}, bf16[4096,1,128]{2,0,1:T(8,128)(2,1)}, bf16[4096,1,1...) while((s32[]{:T(128)}, f32[512,1,128]{0,2,1:T(8,128)S(1)}, ...), condition=%wide.region_6.7_spmd.clone, body=%wide.region_5.6_spmd.clone.sunk | while | flops 338232320 | bytes 6441465 | solution.py:166
  244.6 1.3 fusion.100
  249.7 1.3 fusion.100
  254.7 1.3 fusion.100
  259.8 1.3 fusion.100
  269.9 1.3 fusion.100
  279.3 3.4 collective-permute-start.3
  282.9 3.3 collective-permute-done.3
  286.4 23.3 %all_to_all.67 = bf16[64,2,256]{2,1,0:T(2,128)(2,1)S(1)} all-to-all(bf16[64,2,256]{2,1,0:T(2,128)(2,1)S(1)} %reshape.204), channel_id=1, replica_groups=mesh['seq'=64,'dp'=8] {'seq'}, dimensions={0} | all-to-all | bytes 131072 | tf_op jit(solution)/shard_map/all_to_all | solution.py:175
  309.6 50.0 %all_to_all.68 = bf16[64,64,128]{2,1,0:T(8,128)(2,1)S(1)} all-to-all(bf16[64,64,128]{2,1,0:T(8,128)(2,1)S(1)} %bitcast.196), channel_id=1, replica_groups=mesh['seq'=64,'dp'=8] {'seq'}, dimensions={0} | all-to-all | bytes 2097152 | tf_op jit(solution)/shard_map/all_to_all | solution.py:176
  359.6 6.5 %all-to-all-start.6 = ((bf16[64,64,128]{2,1,0:T(8,128)(2,1)}), bf16[64,64,128]{2,1,0:T(8,128)(2,1)S(1)}, u32[]{:S(2)}, u32[]{:S(2)}) async-start(bf16[64,64,128]{2,1,0:T(8,128)(2,1)} %bitcast.28), calls=%async_computation.6 | async-start | bytes 2097152 | tf_op jit(solution)/shard_map/all_to_all | solution.py:179
  366.2 3.9 fusion.42
  371.1 39.1 %reduce-scatter.2.cloned.1.call-done = bf16[512,64]{0,1:T(8,128)(2,1)} async-done(((bf16[4096,64]{0,1:T(8,128)(2,1)}), bf16[512,64]{0,1:T(8,128)(2,1)}) %reduce-scatter.2.cloned.1.call-update) | async-done | bytes 65552 | tf_op jit(solution)/shard_map/reduce_scatter | solution.py:70
  410.2 1.5 multiply_bitcast_fusion
  (166 shorter events, 54.3 us)
Async XLA Ops:
  7.2 65.3 %copy-start.2 = (bf16[64,512]{1,0:T(8,128)(2,1)S(1)}, bf16[64,512]{1,0:T(8,128)(2,1)}, u32[]{:S(2)}) copy-start(bf16[64,512]{1,0:T(8,128)(2,1)} %param.17) | copy-start | bytes 196612
  7.2 83.4 %copy-start.1 = (bf16[1,128,4096]{2,1,0:T(8,128)(2,1)S(1)}, bf16[1,128,4096]{2,1,0:T(8,128)(2,1)}, u32[]{:S(2)}) copy-start(bf16[1,128,4096]{2,1,0:T(8,128)(2,1)} %param.14) | copy-start | bytes 3145732
  43.7 21.6 %all-to-all-start.3 = ((bf16[64,8,128]{2,1,0:T(8,128)(2,1)}), bf16[64,8,128]{2,1,0:T(8,128)(2,1)S(1)}, u32[]{:S(2)}, u32[]{:S(2)}) async-start(bf16[64,8,128]{2,1,0:T(8,128)(2,1)} %bitcast.18), calls=%async_computation.3 | async-start | bytes 262144 | tf_op jit(solution)/shard_map/all_to_all | solution.py:49
  51.5 40.7 %copy-start.3 = (s32[64]{0:T(128)S(1)}, s32[64]{0:T(128)}, u32[]{:S(2)}) copy-start(s32[64]{0:T(128)} %param.19) | copy-start | bytes 772
  65.2 63.3 %all-to-all-start = ((bf16[64,64,128]{2,1,0:T(8,128)(2,1)}), bf16[64,64,128]{2,1,0:T(8,128)(2,1)S(1)}, u32[]{:S(2)}, u32[]{:S(2)}) async-start(bf16[64,64,128]{2,1,0:T(8,128)(2,1)} %bitcast.1), calls=%async_computation | async-start | bytes 2097152 | tf_op jit(solution)/shard_map/all_to_all | solution.py:50
  71.7 161.5 %all-gather.3.cloned.1.call-start = ((), (), s32[]{:S(2)}) async-start(), calls=%async_computation.9 | async-start | bytes 4259840 | tf_op jit(solution)/shard_map/all_gather | solution.py:65
  87.0 96.0 %collective-permute-start.2 = (bf16[64,4096]{1,0:T(8,128)(2,1)}, bf16[64,4096]{1,0:T(8,128)(2,1)S(1)}, u32[]{:S(2)}, u32[]{:S(2)}) collective-permute-start(bf16[64,4096]{1,0:T(8,128)(2,1)} %all_gather.6), channel_id=1, source_target_pairs={{0,8},{8,0},{16,24},{24,16},{32,40},{40,32},{48,56},{56,48},{64,72... | collective-permute-start | bytes 1572872 | tf_op jit(solution)/shard_map/ppermute | solution.py:16
  128.5 108.9 %all-to-all-start.2 = ((bf16[64,64,128]{2,1,0:T(8,128)(2,1)}), bf16[64,64,128]{2,1,0:T(8,128)(2,1)S(1)}, u32[]{:S(2)}, u32[]{:S(2)}) async-start(bf16[64,64,128]{2,1,0:T(8,128)(2,1)} %bitcast.10), calls=%async_computation.2 | async-start | bytes 2097152 | tf_op jit(solution)/shard_map/all_to_all | solution.py:51
  147.1 5.9 %copy-start = (bf16[4096,1,128]{2,0,1:T(8,128)(2,1)}, bf16[4096,1,128]{2,0,1:T(8,128)(2,1)S(1)}, u32[]{:S(2)}) copy-start(bf16[4096,1,128]{2,0,1:T(8,128)(2,1)S(1)} %get-tuple-element.723) | copy-start | bytes 3145732
  147.1 35.8 %collective-permute-start.1 = (f32[1,512]{1,0:T(1,128)S(1)}, f32[1,512]{1,0:T(1,128)S(1)}, u32[]{:S(2)}, u32[]{:S(2)}) collective-permute-start(f32[1,512]{1,0:T(1,128)S(1)} %get-tuple-element.331), channel_id=1, source_target_pairs={{0,8},{8,0},{16,24},{24,16},{32,40},{40,32},{48,56},{56,48},{64,72... | collective-permute-start | bytes 6152 | tf_op jit(solution)/shard_map/ppermute | solution.py:16
  150.5 32.5 %collective-permute-start = (f32[1,512]{1,0:T(1,128)S(1)}, f32[1,512]{1,0:T(1,128)S(1)}, u32[]{:S(2)}, u32[]{:S(2)}) collective-permute-start(f32[1,512]{1,0:T(1,128)S(1)} %get-tuple-element.330), channel_id=1, source_target_pairs={{0,8},{8,0},{16,24},{24,16},{32,40},{40,32},{48,56},{56,48},{64,72... | collective-permute-start | bytes 6152 | tf_op jit(solution)/shard_map/ppermute | solution.py:16
  279.3 6.9 %collective-permute-start.3 = (bf16[512,64]{1,0:T(8,128)(2,1)S(1)}, bf16[512,64]{1,0:T(8,128)(2,1)S(1)}, u32[]{:S(2)}, u32[]{:S(2)}) collective-permute-start(bf16[512,64]{1,0:T(8,128)(2,1)S(1)} %fusion.57), channel_id=1, source_target_pairs={{0,8},{8,0},{16,24},{24,16},{32,40},{40,32},{48,56},{56,48},{64,72... | collective-permute-start | bytes 196616 | tf_op jit(solution)/shard_map/ppermute | solution.py:16
  359.6 54.1 %all-to-all-start.6 = ((bf16[64,64,128]{2,1,0:T(8,128)(2,1)}), bf16[64,64,128]{2,1,0:T(8,128)(2,1)S(1)}, u32[]{:S(2)}, u32[]{:S(2)}) async-start(bf16[64,64,128]{2,1,0:T(8,128)(2,1)} %bitcast.28), calls=%async_computation.6 | async-start | bytes 2097152 | tf_op jit(solution)/shard_map/all_to_all | solution.py:179
  366.1 44.1 %reduce-scatter.2.cloned.1.call-start = ((), (), s32[]{:S(2)}) async-start(), calls=%async_computation.8 | async-start | bytes 589824 | tf_op jit(solution)/shard_map/reduce_scatter | solution.py:70
Sparse Core Ops, SparseCore 0:
  75.5 157.6 all-gather.2
  370.4 39.8 reduce-scatter.1
where the time goes:
time: 424 us; the launch traced here: 422 us
  waiting for transfers between devices  172 us (41%)
  blocking collectives  122 us (29%)
  matrix products  43.5 us (10%)
  starting transfers between devices  38.5 us (9%)
  local copies, waits for them, and re-layouts  16.6 us (4%)
  other arithmetic  15.3 us (4%)
  between operations  14.4 us (3%)
    all_gather x1, waiting for transfers between devices, on_device(): all_grad = lax.all_gather(grad_rows, 'seq', axis=0, tiled=True)  50.2 us
    all_to_all x1, blocking collectives, on_device(): lax.all_to_all(key_grads.reshape(n_keys, head_cols), 'seq', split_axis=0,...  50 us
    reduce_scatter x1, waiting for transfers between devices, on_device(): lax.psum_scatter(lax.dot_general(all_grad, own_out, contract_rows, prefer...  39.1 us
    all_to_all x1, waiting for transfers between devices, on_device(): lax.all_to_all(split_keys(key_vectors[0]), 'seq', split_axis=0, concat_ax...  36.2 us
    all_to_all x1, blocking collectives, on_device(): lax.all_to_all(spread_rows(queries[0]), 'seq', split_axis=0, concat_axis=...  34 us
    ppermute x4, waiting for transfers between devices, from_partner(): lax.ppermute(value, axis, [(i, i ^ 1 << bit) for i in range(lax.axis_size...  33.1 us
    all_to_all x1, blocking collectives, on_device(): lax.all_to_all(query_send, 'seq', split_axis=0, concat_axis=0, tiled=True)  23.3 us
    all_gather x1, blocking collectives, on_device(): row_block = lax.all_gather(out_weight, 'dp', axis=1, tiled=True)  14.6 us
  transfers between devices with their start and end apart: 10, of which 6 were waited for; matrix products, arithmetic and copies ran while one was open for 7% of the time, Pallas kernels for 0%

commit v1 on v0

v1 whole, which is shorter than its diff:
```python
import math

import jax
import jax.numpy as jnp
from jax import lax
from jax.experimental import pallas as pl
from jax.experimental.pallas import tpu as pltpu
from jax.sharding import PartitionSpec as P

HD = 128
NY, NZ, ND = 4, 16, 8
Q_ROWS = 8
K_ROWS = 128
WIDTH = 4096
COLS = WIDTH // NY
HEADS = COLS // HD
HALF = COLS // 2
GROUP = NY * Q_ROWS
WINDOW = NZ * GROUP
KEYS = NY * K_ROWS
W_ROWS = 64
W_COLS = WIDTH // ND
EXTRA = 128
INV_ROOT = 1.0 / math.sqrt(HD)
LOG2E = 1.0 / math.log(2.0)
LOW = -1e30
HALF_Z = NZ // 2
BF16 = jnp.bfloat16
F32 = jnp.float32
MESH = pl.DeviceIdType.MESH


def dot_nt(a, b):
    return lax.dot_general(a, b, (((1,), (1,)), ((), ())), preferred_element_type=F32)


def dot_tn(a, b):
    return lax.dot_general(a, b, (((0,), (0,)), ((), ())), preferred_element_type=F32)


def dot_nn(a, b):
    return lax.dot_general(a, b, (((1,), (0,)), ((), ())), preferred_element_type=F32)


def fold(block):
    half = block.shape[1] // 2
    return jnp.concatenate([block[:, :half], block[:, half:]], 0)


def unfold(block):
    rows = block.shape[0] // 2
    return jnp.concatenate([block[:rows], block[rows:]], 1)


def kernel(
    q_ref, so_ref, go_ref, k_ref, v_ref, w_ref, qpos_ref,
    gq_ref, gk_ref, gv_ref, gw_ref,
    kb, vb, qg, cg, wg, sog, gg,
    q_out, q_in, so_out, so_in, go_out, go_in, g_out,
    c_out, c_in, prob, row_max, row_lse, scale, delta, lse_a, lse_b,
    gks, gvs, dq, gwp,
    dq_sr, dq_sl, dq_rr, dq_rl, gw_sr, gw_sl, gw_rr, gw_rl, gq_out, gq_in,
    y_send, y_recv, d_send, d_recv, ag_send, ag_recv, l_send, l_recv, rs_send, rs_recv,
    local_sem,
):
    n = lax.axis_index("seq")
    s = lax.axis_index("dp")
    y = lax.div(n, NZ)
    z = lax.rem(n, NZ)

    def at_z(zz):
        return (y * NZ + zz, s)

    def at_y(yy):
        return (yy * NZ + z, s)

    def at_d(ss):
        return (n, ss)

    right = lax.rem(z + 1, NZ)
    left = lax.rem(z + NZ - 1, NZ)
    y_peers = [lax.rem(y + j, NY) for j in range(1, NY)]
    d_peers = [lax.rem(s + j, ND) for j in range(1, ND)]
    z_base = z - lax.rem(z, 4)
    near = [z_base + lax.rem(lax.rem(z, 4) + j, 4) for j in range(1, 4)]
    far = [lax.rem(z + 4 * j, NZ) for j in range(1, 4)]

    barrier = pltpu.get_barrier_semaphore()
    peers = (
        [at_z(right), at_z(left)]
        + [at_y(p) for p in y_peers]
        + [at_d(p) for p in d_peers]
        + [at_z(p) for p in near]
        + [at_z(p) for p in far]
    )
    for p in peers:
        pl.semaphore_signal(barrier, inc=1, device_id=p, device_id_type=MESH)

    wg[pl.ds(z, 1)] = w_ref[...][None]
    go_out[...] = fold(go_ref[...].astype(F32)).astype(BF16)
    q32 = q_ref[...].astype(F32)
    so32 = so_ref[...].astype(F32)
    for i in range(NY):
        q_out[i] = fold(q32[:, i * COLS : (i + 1) * COLS]).astype(BF16)
        so_out[i] = fold(so32[:, i * COLS : (i + 1) * COLS]).astype(BF16)
    go_in[pl.ds(y, 1)] = go_out[...][None]
    q_in[pl.ds(y, 1)] = q_out[pl.ds(y, 1)]
    so_in[pl.ds(y, 1)] = so_out[pl.ds(y, 1)]

    pl.semaphore_wait(barrier, len(peers))

    def remote(src, dst, send, recv, device):
        return pltpu.make_async_remote_copy(
            src_ref=src, dst_ref=dst, send_sem=send, recv_sem=recv,
            device_id=device, device_id_type=MESH,
        )

    def ag_right(buf, stream, k, slot):
        return remote(
            buf.at[slot], buf.at[slot], ag_send.at[stream, k], ag_recv.at[stream, slot], at_z(right)
        )

    def ag_left(buf, stream, k, slot):
        return remote(
            buf.at[slot], buf.at[slot], ag_send.at[stream, HALF_Z + k], ag_recv.at[stream, slot],
            at_z(left),
        )

    def ag_start(buf, stream):
        ag_right(buf, stream, 0, z).start()
        ag_left(buf, stream, 0, z).start()

    def ag_steps(parts):
        @pl.loop(1, HALF_Z - 1)
        def _(k):
            from_left = lax.rem(z + NZ - k, NZ)
            from_right = lax.rem(z + k, NZ)
            for buf, stream in parts:
                ag_right(buf, stream, k, from_left).wait_recv()
                ag_right(buf, stream, k, from_left).start()
                ag_left(buf, stream, k, from_right).wait_recv()
                ag_left(buf, stream, k, from_right).start()

        k = HALF_Z - 1
        for buf, stream in parts:
            slot = lax.rem(z + NZ - k, NZ)
            ag_right(buf, stream, k, slot).wait_recv()
            ag_right(buf, stream, k, slot).start()
            ag_left(buf, stream, k, lax.rem(z + k, NZ)).wait_recv()
        for buf, stream in parts:
            ag_right(buf, stream, 0, lax.rem(z + HALF_Z, NZ)).wait_recv()

    def ag_drain(buf, stream):
        @pl.loop(0, HALF_Z)
        def _(k):
            ag_right(buf, stream, k, z).wait_send()

        @pl.loop(0, HALF_Z - 1)
        def _(k):
            ag_left(buf, stream, k, z).wait_send()

    W_STREAM, Q_STREAM, C_STREAM = 0, 1, 2
    ag_start(wg, W_STREAM)

    def y_copy(kind, j, src_of, dst_of):
        p = y_peers[j]
        return remote(src_of(p), dst_of(y), y_send.at[kind, j], y_recv.at[kind, y], at_y(p))

    def y_wait(kind, dst_of, src_of):
        for j in range(NY - 1):
            p = y_peers[j]
            remote(
                src_of(p), dst_of(p), y_send.at[kind, j], y_recv.at[kind, p], at_y(p)
            ).wait_recv()

    def cols_of(p):
        return pl.ds(pl.multiple_of(p * COLS, COLS), COLS)

    kinds = [
        (lambda p: go_out, lambda p: go_in.at[p]),
        (lambda p: q_out.at[p], lambda p: q_in.at[p]),
        (lambda p: so_out.at[p], lambda p: so_in.at[p]),
        (lambda p: k_ref.at[:, cols_of(p)], lambda p: kb.at[p]),
        (lambda p: v_ref.at[:, cols_of(p)], lambda p: vb.at[p]),
        (lambda p: gvs.at[p], lambda p: gv_ref.at[:, cols_of(p)]),
        (lambda p: gks.at[p], lambda p: gk_ref.at[:, cols_of(p)]),
        (lambda p: gq_out.at[p], lambda p: gq_in.at[p]),
    ]

    def y_start(kind):
        src_of, dst_of = kinds[kind]
        for j in range(NY - 1):
            y_copy(kind, j, src_of, dst_of).start()

    def y_recv_all(kind):
        src_of, dst_of = kinds[kind]
        y_wait(kind, dst_of, src_of)

    def y_drain(kind):
        src_of, dst_of = kinds[kind]
        for j in range(NY - 1):
            y_copy(kind, j, src_of, dst_of).wait_send()

    for kind in range(5):
        y_start(kind)
    own_k = pltpu.make_async_copy(k_ref.at[:, cols_of(y)], kb.at[y], local_sem.at[0])
    own_v = pltpu.make_async_copy(v_ref.at[:, cols_of(y)], vb.at[y], local_sem.at[1])
    own_k.start()
    own_v.start()

    y_recv_all(1)
    rows = [unfold(q_in[i].astype(F32)) for i in range(NY)]
    qg[pl.ds(z, 1)] = jnp.concatenate(rows, 0).astype(BF16)[None]
    ag_start(qg, Q_STREAM)

    def d_copy(kind, j, src, dst):
        return remote(src, dst, d_send.at[kind, j], d_recv.at[kind, s], at_d(d_peers[j]))

    def d_wait(kind, buf):
        for j in range(ND - 1):
            p = d_peers[j]
            remote(
                buf.at[p], buf.at[p], d_send.at[kind, j], d_recv.at[kind, p], at_d(p)
            ).wait_recv()

    y_recv_all(0)
    for d in range(ND):
        top, off = d // (ND // 2), (d % (ND // 2)) * W_COLS
        piece = [
            go_in[i].astype(F32)[top * Q_ROWS : (top + 1) * Q_ROWS, off : off + W_COLS]
            for i in range(NY)
        ]
        g_out[d] = jnp.concatenate(piece, 0).astype(BF16)
    gg[pl.ds(s, 1)] = g_out[pl.ds(s, 1)]
    for j in range(ND - 1):
        d_copy(0, j, g_out.at[d_peers[j]], gg.at[s]).start()

    y_recv_all(2)
    rows = [unfold(so_in[i].astype(F32)) for i in range(NY)]
    sog[pl.ds(s, 1)] = jnp.concatenate(rows, 0).astype(BF16)[None]
    for j in range(ND - 1):
        d_copy(1, j, sog.at[s], sog.at[s]).start()

    ag_steps([(wg, W_STREAM), (qg, Q_STREAM)])

    d_wait(0, gg)

    @pl.loop(0, COLS // 256)
    def _(i):
        block = wg[pl.ds(4 * i, 4)].reshape(256, W_COLS)
        part = dot_nt(gg[...].reshape(ND * GROUP, W_COLS), block)
        c_out[:, :, pl.ds(pl.multiple_of(i * 256, 256), 256)] = part.reshape(
            ND, GROUP, 256
        ).astype(BF16)

    c_in[pl.ds(s, 1)] = c_out[pl.ds(s, 1)]
    for j in range(ND - 1):
        d_copy(2, j, c_out.at[d_peers[j]], c_in.at[s]).start()

    own_k.wait()
    y_recv_all(3)

    @pl.loop(0, HEADS)
    def _(h):
        lanes = pl.ds(pl.multiple_of(h * HD, HD), HD)
        query = qg[:, :, lanes].reshape(WINDOW, HD)
        key_iota = lax.broadcasted_iota(jnp.int32, (K_ROWS, WINDOW), 0)
        scores = []
        for b in range(NY):
            raw = dot_nt(kb[b, :, lanes], query) * (INV_ROOT * LOG2E)
            seen = key_iota <= qpos_ref[...] - (b * NZ + z) * K_ROWS
            scores.append(jnp.where(seen, raw, LOW))
        top = jnp.max(scores[0], 0, keepdims=True)
        for b in range(1, NY):
            top = jnp.maximum(top, jnp.max(scores[b], 0, keepdims=True))
        total = jnp.zeros((1, WINDOW), F32)
        for b in range(NY):
            e = jnp.exp2(scores[b] - top)
            total = total + jnp.sum(e, 0, keepdims=True)
            prob[h, pl.ds(b * K_ROWS, K_ROWS)] = e.astype(BF16)
        row_max[pl.ds(h, 1), :] = top
        row_lse[pl.ds(h, 1), :] = top + jnp.log2(total)

    def lse_copy(level, j, src, dst, zz):
        return remote(src, dst, l_send.at[level, j], l_recv.at[level, j], at_z(zz))

    for j in range(3):
        lse_copy(0, j, row_lse, lse_a.at[j], near[j]).start()

    d_wait(2, c_in)
    context = c_in[0].astype(F32)
    for d in range(1, ND):
        context = context + c_in[d].astype(F32)
    context = context.astype(BF16)
    product = context.astype(F32) * sog[pl.ds(s, 1)].reshape(GROUP, COLS).astype(F32)
    lane = lax.broadcasted_iota(jnp.int32, (GROUP, EXTRA), 1)
    sums = jnp.zeros((GROUP, EXTRA), F32)
    for h in range(HEADS):
        one = jnp.sum(product[:, h * HD : (h + 1) * HD], 1, keepdims=True)
        sums = jnp.where(lax.rem(lane, HEADS) == h, one, sums)
    high = sums.astype(BF16).astype(F32)
    rest = jnp.where(lane < HEADS, high, sums - high)
    cg[pl.ds(z, 1)] = jnp.concatenate([context.astype(F32), rest], 1).astype(BF16)[None]
    ag_start(cg, C_STREAM)

    def joined(first, others):
        most = first
        for o in others:
            most = jnp.maximum(most, o)
        total = jnp.exp2(first - most)
        for o in others:
            total = total + jnp.exp2(o - most)
        return most + jnp.log2(total)

    for j in range(3):
        lse_copy(0, j, row_lse, lse_a.at[j], near[j]).wait()
    row_lse[...] = joined(row_lse[...], [lse_a[j] for j in range(3)])
    for j in range(3):
        lse_copy(1, j, row_lse, lse_b.at[j], far[j]).start()

    d_wait(1, sog)

    @pl.loop(0, COLS // 256)
    def _(i):
        block = sog[:, :, pl.ds(pl.multiple_of(i * 256, 256), 256)].reshape(ND * GROUP, 256)
        part = dot_tn(block, gg[...].reshape(ND * GROUP, W_COLS))
        gwp[pl.ds(4 * i, 4)] = part.reshape(4, W_ROWS, W_COLS)

    for j in range(3):
        lse_copy(1, j, row_lse, lse_b.at[j], far[j]).wait()
    scale[...] = jnp.exp2(row_max[...] - joined(row_lse[...], [lse_b[j] for j in range(3)]))

    ag_steps([(cg, C_STREAM)])
    own_v.wait()
    y_recv_all(4)

    pick_row = lax.broadcasted_iota(jnp.int32, (HEADS, EXTRA), 0)
    pick_lane = lax.broadcasted_iota(jnp.int32, (HEADS, EXTRA), 1)
    pick = jnp.where(
        (lax.rem(pick_lane, HEADS) == pick_row) & (pick_lane < 2 * HEADS), 1.0, 0.0
    ).astype(BF16)
    delta[...] = dot_nt(pick, cg[:, :, COLS:].reshape(WINDOW, EXTRA))

    @pl.loop(0, HEADS)
    def _(h):
        lanes = pl.ds(pl.multiple_of(h * HD, HD), HD)
        query = qg[:, :, lanes].reshape(WINDOW, HD)
        ctx = cg[:, :, lanes].reshape(WINDOW, HD)
        row_scale = scale[pl.ds(h, 1), :]
        row_delta = delta[pl.ds(h, 1), :]
        total = jnp.zeros((WINDOW, HD), F32)
        for b in range(NY):
            attend = prob[h, pl.ds(b * K_ROWS, K_ROWS)].astype(F32) * row_scale
            gvs[b, :, lanes] = dot_nn(attend.astype(BF16), ctx).astype(BF16)
            dprob = dot_nt(vb[b, :, lanes], ctx)
            dscore = (attend * (dprob - row_delta)).astype(BF16)
            gks[b, :, lanes] = (dot_nn(dscore, query) * INV_ROOT).astype(BF16)
            total = total + dot_tn(dscore, kb[b, :, lanes])
        dq[:, :, lanes] = total.reshape(NZ, GROUP, HD)

    y_start(5)
    y_start(6)
    own_gv = pltpu.make_async_copy(gvs.at[y], gv_ref.at[:, cols_of(y)], local_sem.at[2])
    own_gk = pltpu.make_async_copy(gks.at[y], gk_ref.at[:, cols_of(y)], local_sem.at[3])
    own_gv.start()
    own_gk.start()

    parts = [
        (dq, dq_sr, dq_sl, dq_rr, dq_rl, 0),
        (gwp, gw_sr, gw_sl, gw_rr, gw_rl, 1),
    ]

    def rs_right(part, k):
        _, sr, _, rr, _, stream = part
        return remote(
            sr.at[k], rr.at[k], rs_send.at[stream, k], rs_recv.at[stream, k], at_z(right)
        )

    def rs_left(part, k):
        _, _, sl, _, rl, stream = part
        return remote(
            sl.at[k], rl.at[k], rs_send.at[stream, HALF_Z + k], rs_recv.at[stream, HALF_Z + k],
            at_z(left),
        )

    for part in parts:
        own, sr, sl = part[:3]
        sr[0] = own[pl.ds(lax.rem(z + HALF_Z, NZ), 1)][0].astype(BF16)
        rs_right(part, 0).start()
        sl[0] = own[pl.ds(lax.rem(z + NZ - (HALF_Z - 1), NZ), 1)][0].astype(BF16)
        rs_left(part, 0).start()

    @pl.loop(1, HALF_Z - 1)
    def _(k):
        for part in parts:
            own, sr, sl, rr, rl, _ = part
            rs_right(part, k - 1).wait_recv()
            mine = own[pl.ds(lax.rem(z + HALF_Z - k, NZ), 1)]
            sr[pl.ds(k, 1)] = (rr[pl.ds(k - 1, 1)].astype(F32) + mine).astype(BF16)
            rs_right(part, k).start()
            rs_left(part, k - 1).wait_recv()
            mine = own[pl.ds(lax.rem(z + NZ - (HALF_Z - 1) + k, NZ), 1)]
            sl[pl.ds(k, 1)] = (rl[pl.ds(k - 1, 1)].astype(F32) + mine).astype(BF16)
            rs_left(part, k).start()

    k = HALF_Z - 1
    for part in parts:
        own, sr, sl, rr, rl, _ = part
        rs_right(part, k - 1).wait_recv()
        mine = own[pl.ds(lax.rem(z + HALF_Z - k, NZ), 1)][0]
        sr[k] = (rr[k - 1].astype(F32) + mine).astype(BF16)
        rs_right(part, k).start()

    def rs_result(part):
        own, _, _, rr, rl, _ = part
        rs_left(part, HALF_Z - 2).wait_recv()
        rs_right(part, HALF_Z - 1).wait_recv()
        return (
            own[pl.ds(z, 1)][0] + rr[HALF_Z - 1].astype(F32) + rl[HALF_Z - 2].astype(F32)
        )

    query_grad = rs_result(parts[0]) * INV_ROOT
    for i in range(NY):
        gq_out[i] = fold(query_grad[i * Q_ROWS : (i + 1) * Q_ROWS]).astype(BF16)
    gq_in[pl.ds(y, 1)] = gq_out[pl.ds(y, 1)]
    y_start(7)
    gw_ref[...] = rs_result(parts[1]) * (1.0 / (ND * WINDOW))
    y_recv_all(7)
    for i in range(NY):
        gq_ref[:, i * COLS : (i + 1) * COLS] = unfold(gq_in[i].astype(F32)).astype(BF16)

    for buf, stream in ((wg, W_STREAM), (qg, Q_STREAM), (cg, C_STREAM)):
        ag_drain(buf, stream)
    for j in range(ND - 1):
        d_copy(0, j, g_out.at[d_peers[j]], gg.at[s]).wait_send()
        d_copy(1, j, sog.at[s], sog.at[s]).wait_send()
        d_copy(2, j, c_out.at[d_peers[j]], c_in.at[s]).wait_send()
    for part in parts:

        @pl.loop(0, HALF_Z)
        def _(k):
            rs_right(part, k).wait_send()

        @pl.loop(0, HALF_Z - 1)
        def _(k):
            rs_left(part, k).wait_send()

    y_recv_all(5)
    y_recv_all(6)
    own_gv.wait()
    own_gk.wait()
    for kind in range(8):
        y_drain(kind)


def on_device(
    queries, key_vectors, value_vectors, saved_out, grad_out, out_weight, window_start, block_order
):
    blocks = block_order.reshape(NY, NZ).T.reshape(NZ * NY, 1) * Q_ROWS
    query_pos = window_start[0] + blocks + jnp.arange(Q_ROWS, dtype=jnp.int32)[None, :]
    vmem = pl.BlockSpec(memory_space=pltpu.VMEM)
    hbm = pl.BlockSpec(memory_space=pl.ANY)

    def buf(*shape, dtype=BF16):
        return pltpu.VMEM(shape, dtype)

    dma = pltpu.SemaphoreType.DMA
    scratch = [
        buf(NY, K_ROWS, COLS), buf(NY, K_ROWS, COLS),
        buf(NZ, GROUP, COLS), buf(NZ, GROUP, COLS + EXTRA), buf(NZ, W_ROWS, W_COLS),
        buf(ND, GROUP, COLS), buf(ND, GROUP, W_COLS),
        buf(NY, 2 * Q_ROWS, HALF), buf(NY, 2 * Q_ROWS, HALF),
        buf(NY, 2 * Q_ROWS, HALF), buf(NY, 2 * Q_ROWS, HALF),
        buf(2 * Q_ROWS, WIDTH // 2), buf(NY, 2 * Q_ROWS, WIDTH // 2),
        buf(ND, GROUP, W_COLS),
        buf(ND, GROUP, COLS), buf(ND, GROUP, COLS),
        buf(HEADS, KEYS, WINDOW),
        buf(HEADS, WINDOW, dtype=F32), buf(HEADS, WINDOW, dtype=F32),
        buf(HEADS, WINDOW, dtype=F32), buf(HEADS, WINDOW, dtype=F32),
        buf(3, HEADS, WINDOW, dtype=F32), buf(3, HEADS, WINDOW, dtype=F32),
        buf(NY, K_ROWS, COLS), buf(NY, K_ROWS, COLS),
        buf(NZ, GROUP, COLS, dtype=F32), buf(NZ, W_ROWS, W_COLS, dtype=F32),
        buf(HALF_Z, GROUP, COLS), buf(HALF_Z, GROUP, COLS),
        buf(HALF_Z, GROUP, COLS), buf(HALF_Z, GROUP, COLS),
        buf(HALF_Z, W_ROWS, W_COLS), buf(HALF_Z, W_ROWS, W_COLS),
        buf(HALF_Z, W_ROWS, W_COLS), buf(HALF_Z, W_ROWS, W_COLS),
        buf(NY, 2 * Q_ROWS, HALF), buf(NY, 2 * Q_ROWS, HALF),
        dma((8, NY - 1)), dma((8, NY)),
        dma((3, ND - 1)), dma((3, ND)),
        dma((3, NZ)), dma((3, NZ)),
        dma((2, 3)), dma((2, 3)),
        dma((2, NZ)), dma((2, NZ)),
        dma((4,)),
    ]
    outs = pl.pallas_call(
        kernel,
        out_shape=(
            jax.ShapeDtypeStruct((Q_ROWS, WIDTH), BF16),
            jax.ShapeDtypeStruct((K_ROWS, WIDTH), BF16),
            jax.ShapeDtypeStruct((K_ROWS, WIDTH), BF16),
            jax.ShapeDtypeStruct((W_ROWS, W_COLS), F32),
        ),
        in_specs=[vmem, vmem, vmem, hbm, hbm, vmem, vmem],
        out_specs=(vmem, hbm, hbm, vmem),
        scratch_shapes=scratch,
        compiler_params=pltpu.CompilerParams(
            collective_id=0, has_side_effects=True, vmem_limit_bytes=48 * 1024 * 1024
        ),
        name="attention_backward",
    )(
        queries[0], saved_out[0], grad_out[0], key_vectors[0], value_vectors[0], out_weight,
        query_pos.reshape(1, WINDOW),
    )
    return (outs[0][None], outs[1][None], outs[2][None], outs[3])


def solution(mesh):
    rows = P("dp", "seq", None)
    return jax.shard_map(
        on_device,
        mesh=mesh,
        in_specs=(rows, rows, rows, rows, rows, P("seq", "dp"), P("dp"), P()),
        out_specs=(rows, rows, rows, P("seq", "dp")),
        check_vma=False,
    )
```

time: 424 us -> 155 us (0.37)
  waiting for transfers between devices: 172 us -> 0 us
  Pallas kernels: 0 us -> 144 us
  blocking collectives: 122 us -> 0 us
  matrix products: 43.5 us -> 0 us
  starting transfers between devices: 38.5 us -> 0 us
  other arithmetic: 15.3 us -> 0.73 us
  between operations: 14.4 us -> 1.35 us
  local copies, waits for them, and re-layouts: 16.6 us -> 8.55 us
    pallas_call x0 -> x1, Pallas kernels: none -> 144 us  [on_device(): pl.pallas_call(kernel, out_shape=(jax.ShapeDtypeStruct((Q_ROWS, WIDTH), B...]
    all_to_all x3 -> x0, blocking collectives: 107 us -> none  [the longest x1 50 us: on_device(): lax.all_to_all(key_grads.reshape(n_keys, head_cols), 'seq', split_axis=0,...]
    all_gather x1 -> x0, waiting for transfers between devices: 50.2 us -> none  [on_device(): all_grad = lax.all_gather(grad_rows, 'seq', axis=0, tiled=True)]
    all_to_all x4 -> x0, waiting for transfers between devices: 48.6 us -> none  [the longest x1 36.2 us: on_device(): lax.all_to_all(split_keys(key_vectors[0]), 'seq', split_axis=0, concat_ax...]
    dot_general x50 -> x0, matrix products: 43.5 us -> none  [the longest x16 13.2 us: block_scores(): jnp.einsum('qhd,khd->hqk', query_heads, key_block, preferred_element_type...]
    reduce_scatter x1 -> x0, waiting for transfers between devices: 39.1 us -> none  [on_device(): lax.psum_scatter(lax.dot_general(all_grad, own_out, contract_rows, prefer...]
    ppermute x4 -> x0, waiting for transfers between devices: 33.1 us -> none  [from_partner(): lax.ppermute(value, axis, [(i, i ^ 1 << bit) for i in range(lax.axis_size...]
    all_to_all x4 -> x0, starting transfers between devices: 25.8 us -> none  [the longest x1 6.52 us: on_device(): lax.all_to_all(value_grads.reshape(n_keys, head_cols), 'seq', split_axis=...]
  transfers between devices with their start and end apart: 10 -> 0, of which waited for: 6 -> 0; matrix products, arithmetic and copies ran while one was open for 7% -> 0% of each run, Pallas kernels for 0% -> 0%
where the time goes in v1:
time: 155 us
  Pallas kernels  144 us (93%)
  local copies, waits for them, and re-layouts  8.55 us (6%)
    pallas_call x1, Pallas kernels, on_device(): pl.pallas_call(kernel, out_shape=(jax.ShapeDtypeStruct((Q_ROWS, WIDTH), B...  144 us
    unnamed x16, local copies, waits for them, and re-layouts  8.19 us

profile of v1, /device:TPU:24, one launch (start us, length us, event | category | flops | bytes accessed | tf_op | source)
XLA Modules:
  0.0 155.0 jit_solution(8087362377069703456)
XLA Ops:
  0.6 0.0 copy-start.2
  1.3 0.7 multiply_add_fusion
  2.0 0.1 add.45
  2.1 0.1 copy.13
  2.1 0.1 add.47
  2.2 0.1 iota_add_fusion
  2.3 0.1 add.51.qpos_ref
  2.4 0.0 copy-done.2
  2.4 0.0 copy-start
  2.4 1.2 copy-done
  3.7 0.0 copy-start.1
  3.7 1.2 copy-done.1
  4.9 0.0 copy-start.3
  4.9 0.8 copy-done.3
  5.7 0.0 copy-start.4
  5.7 0.8 copy-done.4
  6.6 0.0 copy-start.5
  6.6 0.8 copy-done.5
  7.4 144.4 %attention_backward.1 = (bf16[8,4096]{1,0:T(8,128)(2,1)S(1)}, bf16[128,4096]{1,0:T(8,128)(2,1)S(1)}, bf16[128,4096]{1,0:T(8,128)(2,1)S(1)}, f32[64,512]{1,0:T(8,128)S(1)}) custom-call(bf16[8,4096]{1,0:T(8,128)(2,1)S(1)} %bitcast.15, bf16[8,4096]{1,0:T(8,128)(2,1)S(1)} %bitcast.16, bf16[8,4096]{1,0:T(8,128)(2,1)S(1)} %bitcast.17, ...), custom_call_target="tpu_custom_call" | custom-call | tf_op jit(solution)/shard_map/attention_backward/pallas_call | solution.py:495
  151.8 0.6 copy.19
  152.4 1.0 copy.20
  153.4 1.0 copy.21
  154.3 0.7 copy.22
Async XLA Ops:
  0.6 1.8 %copy-start.2 = (bf16[1,8,4096]{2,1,0:T(8,128)(2,1)S(1)}, bf16[1,8,4096]{2,1,0:T(8,128)(2,1)}, u32[]{:S(2)}) copy-start(bf16[1,8,4096]{2,1,0:T(8,128)(2,1)} %param.8) | copy-start | bytes 196612
  2.4 1.2 copy-start
  3.7 1.2 copy-start.1
  4.9 0.8 copy-start.3
  5.7 0.8 copy-start.4
  6.6 0.8 copy-start.5

commit v2 on v1

v2 whole, which is shorter than its diff:
```python
import math

import jax
import jax.numpy as jnp
from jax import lax
from jax.experimental import pallas as pl
from jax.experimental.pallas import tpu as pltpu
from jax.sharding import PartitionSpec as P

HD = 128
NY, NZ, ND = 4, 16, 8
Q_ROWS = 8
K_ROWS = 128
WIDTH = 4096
COLS = WIDTH // NY
HEADS = COLS // HD
HALF = COLS // 2
GROUP = NY * Q_ROWS
WINDOW = NZ * GROUP
KEYS = NY * K_ROWS
W_ROWS = 64
W_COLS = WIDTH // ND
INV_ROOT = 1.0 / math.sqrt(HD)
LOG2E = 1.0 / math.log(2.0)
LOW = -1e30
HALF_Z = NZ // 2
CHUNKS = 4
CHUNK = COLS // CHUNKS
BLOCK = WINDOW // CHUNKS
SLOT = HEADS * GROUP + 2 * HEADS
NEAR = 4
JUMP = 5
VMEM_BYTES = 64 * 1024 * 1024
BF16 = jnp.bfloat16
F32 = jnp.float32
MESH = pl.DeviceIdType.MESH


def dot_nt(a, b):
    return lax.dot_general(a, b, (((1,), (1,)), ((), ())), preferred_element_type=F32)


def dot_tn(a, b):
    return lax.dot_general(a, b, (((0,), (0,)), ((), ())), preferred_element_type=F32)


def dot_nn(a, b):
    return lax.dot_general(a, b, (((1,), (0,)), ((), ())), preferred_element_type=F32)


def fold(block):
    half = block.shape[1] // 2
    return jnp.concatenate([block[:, :half], block[:, half:]], 0)


def unfold(block):
    rows = block.shape[0] // 2
    return jnp.concatenate([block[:rows], block[rows:]], 1)


def kernel(
    q_ref, so_ref, go_ref, k_ref, v_ref, w_ref, order_ref, start_ref,
    gq_ref, gk_ref, gv_ref, gw_ref,
    q_own, so_own, go_own,
    kb, vb, qg, cg, wg, sog, gg,
    q_out, q_in, so_out, so_in, go_out, go_in, g_out,
    c_out, c_in, prob, query_pos, row_max, lse_own, lse_near, lse_a, lse_b, scale, delta,
    gvs, gks, dq, gwp, gw_out,
    dq_send, dq_recv, gw_sr, gw_sl, gw_rr, gw_rl, gq_out, gq_in, gq_all,
    y_send, y_recv, d_send, d_recv, ag_send, ag_recv, l_send, l_recv,
    dq_ssem, dq_rsem, gw_ssem, gw_rsem, local_sem,
):
    n = lax.axis_index("seq")
    s = lax.axis_index("dp")
    y = lax.div(n, NZ)
    z = lax.rem(n, NZ)

    def at_y(yy):
        return (yy * NZ + z, s)

    def at_d(ss):
        return (n, ss)

    def z_off(j):
        return lax.rem(z + (j + NZ), NZ)

    def at_z(j):
        return (y * NZ + z_off(j), s)

    y_peers = [lax.rem(y + j, NY) for j in range(1, NY)]
    d_peers = [lax.rem(s + j, ND) for j in range(1, ND)]
    z_low = lax.rem(z, 4)
    z_high = lax.div(z, 4)

    def nth_block(i):
        turn = i + lax.div(i, 2) - 2 * lax.div(i, 3)
        toward = 2 * lax.div(z_low, 2) - 1
        return lax.rem(z_high + 8 + toward * turn, CHUNKS)

    near = [(y * NZ + z - z_low + lax.rem(z_low + j, 4), s) for j in range(1, 4)]
    far = [at_z(4 * j) for j in range(1, 4)]

    barrier = pltpu.get_barrier_semaphore()
    peers = (
        [at_z(1), at_z(-1), at_z(JUMP), at_z(-JUMP)]
        + [at_y(p) for p in y_peers]
        + [at_d(p) for p in d_peers]
        + near
        + far
    )
    for p in peers:
        pl.semaphore_signal(barrier, inc=1, device_id=p, device_id_type=MESH)

    def cols_of(p):
        return pl.ds(pl.multiple_of(p * COLS, COLS), COLS)

    loads = [
        pltpu.make_async_copy(src, dst, local_sem.at[i])
        for i, (src, dst) in enumerate([
            (go_ref, go_own),
            (q_ref, q_own),
            (so_ref, so_own),
            (w_ref, wg.at[z]),
            (k_ref.at[:, cols_of(y)], kb.at[y]),
            (v_ref.at[:, cols_of(y)], vb.at[y]),
        ])
    ]
    for load in loads:
        load.start()

    row = lax.broadcasted_iota(jnp.int32, (NY * NZ, WINDOW), 0)
    place = lax.broadcasted_iota(jnp.int32, (NY * NZ, WINDOW), 1)
    holder = ((place >> 3) & (NY - 1)) * NZ + (place >> 5)
    select = jnp.where(row == holder, 1.0, 0.0).astype(BF16)
    order = jnp.broadcast_to(order_ref[...].astype(F32), (8, NY * NZ)).astype(BF16)
    inside = (lax.broadcasted_iota(jnp.int32, (8, WINDOW), 1) & (Q_ROWS - 1)).astype(F32)
    query_pos[...] = dot_nn(order, select) * Q_ROWS + inside + start_ref[0].astype(F32)

    loads[0].wait()
    go_out[...] = fold(go_own[...].astype(F32)).astype(BF16)
    loads[1].wait()
    loads[2].wait()
    q32 = q_own[...].astype(F32)
    so32 = so_own[...].astype(F32)
    for i in range(NY):
        q_out[i] = fold(q32[:, i * COLS : (i + 1) * COLS]).astype(BF16)
        so_out[i] = fold(so32[:, i * COLS : (i + 1) * COLS]).astype(BF16)
    go_in[pl.ds(y, 1)] = go_out[...][None]
    q_in[pl.ds(y, 1)] = q_out[pl.ds(y, 1)]
    so_in[pl.ds(y, 1)] = so_out[pl.ds(y, 1)]
    loads[3].wait()

    pl.semaphore_wait(barrier, len(peers))

    def remote(src, dst, send, recv, device):
        return pltpu.make_async_remote_copy(
            src_ref=src, dst_ref=dst, send_sem=send, recv_sem=recv,
            device_id=device, device_id_type=MESH,
        )

    streams = [wg, qg, cg]

    def z_send(stream, sem, distance, hop):
        buf, slot = streams[stream], z_off(-distance)
        return remote(
            buf.at[slot], buf.at[slot], ag_send.at[stream, sem], ag_recv.at[stream, slot], at_z(hop)
        )

    def z_arrived(stream, distance):
        z_send(stream, 0, distance, 1).wait_recv()

    z_sends = {}

    def z_go(stream, distance, hop):
        sem = z_sends.get(stream, 0)
        z_sends[stream] = sem + 1
        z_send(stream, sem, distance, hop).start()

    def ring_start(stream):
        z_go(stream, 0, 1)
        z_go(stream, 0, -1)

    def ring_step(stream, k):
        z_arrived(stream, k)
        if k < HALF_Z:
            z_go(stream, k, 1)
            z_arrived(stream, -k)
            if k < HALF_Z - 1:
                z_go(stream, -k, -1)

    def wave_start(stream):
        z_go(stream, 0, 1)
        z_go(stream, 0, -1)
        z_go(stream, 0, JUMP)
        z_go(stream, 0, -JUMP)

    def wave_near(stream, k):
        for sign in (1, -1):
            z_arrived(stream, sign * k)
            if k < NEAR:
                z_go(stream, sign * k, sign)

    def wave_far(stream, k):
        for sign, last in ((1, HALF_Z), (-1, HALF_Z - 1)):
            distance = NEAR + k
            if distance <= last:
                z_arrived(stream, sign * distance)
            if distance < last:
                z_go(stream, sign * distance, sign)

    def z_drain(stream):
        @pl.loop(0, z_sends[stream])
        def _(sem):
            z_send(stream, sem, 0, 1).wait_send()

    W, Q, C = 0, 1, 2

    kinds = [
        (lambda p: go_out, lambda p: go_in.at[p]),
        (lambda p: q_out.at[p], lambda p: q_in.at[p]),
        (lambda p: so_out.at[p], lambda p: so_in.at[p]),
        (lambda p: k_ref.at[:, cols_of(p)], lambda p: kb.at[p]),
        (lambda p: v_ref.at[:, cols_of(p)], lambda p: vb.at[p]),
        (lambda p: gvs.at[p], lambda p: gv_ref.at[:, cols_of(p)]),
        (lambda p: gks.at[p], lambda p: gk_ref.at[:, cols_of(p)]),
        (lambda p: gq_out.at[p], lambda p: gq_in.at[p]),
    ]
    GV, GK, GQ = 5, 6, 7

    def y_copy(kind, j, slot):
        src_of, dst_of = kinds[kind]
        p = y_peers[j]
        return remote(
            src_of(p), dst_of(slot), y_send.at[kind, j], y_recv.at[kind, slot], at_y(p)
        )

    def y_start(kind):
        for j in range(NY - 1):
            y_copy(kind, j, y).start()

    def y_arrived(kind):
        for j in range(NY - 1):
            y_copy(kind, j, y_peers[j]).wait_recv()

    def y_drain(kind):
        for j in range(NY - 1):
            y_copy(kind, j, y).wait_send()

    d_sends = []

    def d_start(kind, src_of, buf):
        for j in range(ND - 1):
            p = d_peers[j]
            copy = remote(
                src_of(p), buf.at[s], d_send.at[kind, j], d_recv.at[kind, s], at_d(p)
            )
            copy.start()
            d_sends.append(copy)

    def d_arrived(kind, buf):
        for j in range(ND - 1):
            p = d_peers[j]
            remote(
                buf.at[p], buf.at[p], d_send.at[kind, j], d_recv.at[kind, p], at_d(p)
            ).wait_recv()

    def partial_context(i):
        block = wg[pl.ds(4 * nth_block(i), 4)].reshape(CHUNK, W_COLS)
        part = dot_nt(gg[...].reshape(ND * GROUP, W_COLS), block)
        c_out[i] = part.reshape(ND, GROUP, CHUNK).astype(BF16)
        c_in[i, pl.ds(s, 1)] = c_out[i, pl.ds(s, 1)]
        d_start(2 + i, lambda p: c_out.at[i, p], c_in.at[i])

    def gw_right(k):
        return remote(gw_sr.at[k], gw_rr.at[k], gw_ssem.at[k], gw_rsem.at[k], at_z(1))

    def gw_left(k):
        i = HALF_Z + k
        return remote(gw_sl.at[k], gw_rl.at[k], gw_ssem.at[i], gw_rsem.at[i], at_z(-1))

    def gw_step(k):
        mine = gwp[pl.ds(z_off(HALF_Z - k), 1)][0]
        if k > 0:
            gw_right(k - 1).wait_recv()
            mine = mine + gw_rr[k - 1].astype(F32)
        gw_sr[k] = mine.astype(BF16)
        gw_right(k).start()
        if k < HALF_Z - 1:
            mine = gwp[pl.ds(z_off(k + 1 - HALF_Z), 1)][0]
            if k > 0:
                gw_left(k - 1).wait_recv()
                mine = mine + gw_rl[k - 1].astype(F32)
            gw_sl[k] = mine.astype(BF16)
            gw_left(k).start()

    gw_store = pltpu.make_async_copy(gw_out, gw_ref, local_sem.at[6])

    def gw_end():
        gw_left(HALF_Z - 2).wait_recv()
        gw_right(HALF_Z - 1).wait_recv()
        total = (
            gwp[pl.ds(z, 1)][0]
            + gw_rr[HALF_Z - 1].astype(F32)
            + gw_rl[HALF_Z - 2].astype(F32)
        )
        gw_out[...] = total * (1.0 / (ND * WINDOW))
        gw_store.start()

    def softmax_head(h):
        lanes = pl.ds(pl.multiple_of(h * HD, HD), HD)
        query = qg[:, :, lanes].reshape(WINDOW, HD)
        key_place = lax.broadcasted_iota(jnp.int32, (K_ROWS, WINDOW), 0).astype(F32)
        scores = []
        for b in range(NY):
            raw = dot_nt(kb[b, :, lanes], query) * (INV_ROOT * LOG2E)
            first_key = ((b * NZ + z) * K_ROWS).astype(F32)
            seen = key_place <= query_pos[0:1, :] - first_key
            scores.append(jnp.where(seen, raw, LOW))
        top = jnp.max(scores[0], 0, keepdims=True)
        for b in range(1, NY):
            top = jnp.maximum(top, jnp.max(scores[b], 0, keepdims=True))
        total = jnp.zeros((1, WINDOW), F32)
        for b in range(NY):
            e = jnp.exp2(scores[b] - top)
            total = total + jnp.sum(e, 0, keepdims=True)
            prob[h, b * K_ROWS : (b + 1) * K_ROWS] = e.astype(BF16)
        row_max[pl.ds(h, 1), :] = top
        lse_own[pl.ds(h, 1), :] = top + jnp.log2(total)

    def lse_copy(level, j):
        src, dst = ((lse_own, lse_a), (lse_near, lse_b))[level]
        i = level * 3 + j
        return remote(src, dst.at[j], l_send.at[i], l_recv.at[i], (near, far)[level][j])

    def joined(first, others):
        most = first
        for o in others:
            most = jnp.maximum(most, o)
        total = jnp.exp2(first - most)
        for o in others:
            total = total + jnp.exp2(o - most)
        return most + jnp.log2(total)

    def lse_start():
        for j in range(3):
            lse_copy(0, j).start()

    def lse_next():
        for j in range(3):
            lse_copy(0, j).wait()
        lse_near[...] = joined(lse_own[...], [lse_a[j] for j in range(3)])
        for j in range(3):
            lse_copy(1, j).start()

    def lse_end():
        for j in range(3):
            lse_copy(1, j).wait()
        lse = joined(lse_near[...], [lse_b[j] for j in range(3)])
        scale[...] = jnp.exp2(row_max[...] - lse)

    def both(k):
        ring_step(W, k)
        ring_step(Q, k)

    y_start(1)
    y_start(0)
    ring_start(W)
    for kind in range(2, 5):
        y_start(kind)

    y_arrived(1)
    rows = [unfold(q_in[i].astype(F32)) for i in range(NY)]
    qg[pl.ds(z, 1)] = jnp.concatenate(rows, 0).astype(BF16)[None]
    ring_start(Q)

    y_arrived(0)
    for d in range(ND):
        top, off = d // (ND // 2), (d % (ND // 2)) * W_COLS
        piece = [
            go_in[i].astype(F32)[top * Q_ROWS : (top + 1) * Q_ROWS, off : off + W_COLS]
            for i in range(NY)
        ]
        g_out[d] = jnp.concatenate(piece, 0).astype(BF16)
    gg[pl.ds(s, 1)] = g_out[pl.ds(s, 1)]
    d_start(0, lambda p: g_out.at[p], gg)

    both(1)
    y_arrived(2)
    rows = [unfold(so_in[i].astype(F32)) for i in range(NY)]
    sog[pl.ds(s, 1)] = jnp.concatenate(rows, 0).astype(BF16)[None]
    d_start(1, lambda p: sog.at[s], sog)

    both(2)
    both(3)
    d_arrived(0, gg)
    partial_context(0)
    both(4)
    both(5)
    partial_context(1)
    both(6)
    d_arrived(1, sog)
    for i in range(CHUNKS):
        block = sog[:, :, i * CHUNK : (i + 1) * CHUNK].reshape(ND * GROUP, CHUNK)
        piece = dot_tn(block, gg[...].reshape(ND * GROUP, W_COLS))
        gwp[4 * i : 4 * i + 4] = piece.reshape(4, W_ROWS, W_COLS)
    both(7)
    partial_context(2)
    ring_step(W, 8)
    partial_context(3)
    ring_step(Q, 8)

    loads[4].wait()
    y_arrived(3)

    @pl.loop(0, HEADS, unroll=2)
    def _(h):
        softmax_head(h)

    lse_start()

    lane = lax.broadcasted_iota(jnp.int32, (GROUP, HD), 1)
    sums = jnp.zeros((GROUP, HD), F32)
    for i in range(CHUNKS):
        d_arrived(2 + i, c_in.at[i])
        context = c_in[i, 0].astype(F32)
        for d in range(1, ND):
            context = context + c_in[i, d].astype(F32)
        context = context.astype(BF16)
        chunk = nth_block(i)
        lanes = pl.ds(pl.multiple_of(chunk * CHUNK, CHUNK), CHUNK)
        product = context.astype(F32) * sog[pl.ds(s, 1), :, lanes][0].astype(F32)
        for j in range(CHUNK // HD):
            h = chunk * (CHUNK // HD) + j
            own = slice(j * HD, (j + 1) * HD)
            cg[pl.ds(z, 1), pl.ds(pl.multiple_of(h * GROUP, GROUP), GROUP), :] = context[:, own][None]
            one = jnp.sum(product[:, own], 1, keepdims=True)
            sums = jnp.where((lane & (HEADS - 1)) == h, one, sums)
    high = sums.astype(BF16).astype(F32)
    rest = jnp.where(lane < HEADS, high, sums - high).astype(BF16)
    row = lax.broadcasted_iota(jnp.int32, (GROUP, HD), 0)
    place = jnp.where(lane == row + z_low * GROUP, 1.0, 0.0).astype(BF16)
    cg[pl.ds(z, 1), HEADS * GROUP :, :] = dot_tn(rest, place)[: 2 * HEADS].astype(BF16)[None]
    wave_start(C)
    wave_near(C, 1)
    lse_next()
    wave_near(C, 2)
    gw_step(0)
    wave_far(C, 1)
    wave_near(C, 3)
    gw_step(1)
    wave_far(C, 2)
    lse_end()
    wave_near(C, 4)
    gw_step(2)
    wave_far(C, 3)
    gw_step(3)
    wave_far(C, 4)
    loads[5].wait()
    y_arrived(4)

    chains = [(1, HALF_Z, 4), (-1, HALF_Z - 1, 3), (1, NEAR, 4), (-1, NEAR, 4)]

    def dq_copy(c, k):
        sign, reach, length = chains[c]
        hop = sign * JUMP if reach > NEAR and k == length - 1 else sign
        i = 4 * c + k
        return remote(dq_send.at[i], dq_recv.at[i], dq_ssem.at[i], dq_rsem.at[i], at_z(hop))

    def dq_step(k):
        for c, (sign, reach, length) in enumerate(chains):
            if k < length:
                mine = dq[pl.ds(z_off(sign * (reach - k)), 1)][0]
                if k > 0:
                    dq_copy(c, k - 1).wait_recv()
                    mine = mine + dq_recv[4 * c + k - 1].astype(F32)
                dq_send[4 * c + k] = mine.astype(BF16)
                dq_copy(c, k).start()

    def dq_end():
        total = dq[pl.ds(z, 1)][0]
        for c in (2, 3, 0, 1):
            last = chains[c][2] - 1
            dq_copy(c, last).wait_recv()
            total = total + dq_recv[4 * c + last].astype(F32)
        total = total * INV_ROOT
        for i in range(NY):
            gq_out[i] = fold(total[i * Q_ROWS : (i + 1) * Q_ROWS]).astype(BF16)
        gq_in[pl.ds(y, 1)] = gq_out[pl.ds(y, 1)]
        y_start(GQ)

    for i in range(CHUNKS):
        tile = cg[4 * i : 4 * i + 4, HEADS * GROUP :, :].astype(F32)
        tile = tile[0] + tile[1] + tile[2] + tile[3]
        delta[:, i * BLOCK : (i + 1) * BLOCK] = tile[:HEADS] + tile[HEADS:]

    @pl.loop(0, HEADS, unroll=2)
    def _(h):
        lanes = pl.ds(pl.multiple_of(h * HD, HD), HD)
        query = qg[:, :, lanes].reshape(WINDOW, HD)
        head_rows = pl.ds(pl.multiple_of(h * GROUP, GROUP), GROUP)
        ctx = cg[:, head_rows, :].reshape(WINDOW, HD)
        attend = prob[h].astype(F32) * scale[pl.ds(h, 1), :]
        value_grad = dot_nn(attend.astype(BF16), ctx)
        dprob = dot_nt(vb[:, :, lanes].reshape(KEYS, HD), ctx)
        dscore = (attend * (dprob - delta[pl.ds(h, 1), :])).astype(BF16)
        key_grad = dot_nn(dscore, query) * INV_ROOT
        query_grad = dot_tn(dscore, kb[:, :, lanes].reshape(KEYS, HD))
        gvs[:, :, lanes] = value_grad.astype(BF16).reshape(NY, K_ROWS, HD)
        gks[:, :, lanes] = key_grad.astype(BF16).reshape(NY, K_ROWS, HD)
        dq[:, :, lanes] = query_grad.reshape(NZ, GROUP, HD)

    dq_step(0)
    y_start(GV)
    y_start(GK)
    own_stores = [
        pltpu.make_async_copy(src.at[y], dst.at[:, cols_of(y)], local_sem.at[7 + i])
        for i, (src, dst) in enumerate([(gvs, gv_ref), (gks, gk_ref)])
    ]
    for store in own_stores:
        store.start()
    dq_step(1)
    gw_step(4)
    z_drain(W)
    z_drain(Q)
    dq_step(2)
    gw_step(5)
    z_drain(C)
    dq_step(3)
    gw_step(6)
    for copy in d_sends:
        copy.wait_send()
    for kind in range(5):
        y_drain(kind)
    gw_step(7)
    dq_end()
    gw_end()
    for k in range(HALF_Z):
        gw_right(k).wait_send()
    for k in range(HALF_Z - 1):
        gw_left(k).wait_send()
    for c, (_, _, length) in enumerate(chains):
        for k in range(length):
            dq_copy(c, k).wait_send()
    y_arrived(GQ)
    for i in range(NY):
        gq_all[:, i * COLS : (i + 1) * COLS] = unfold(gq_in[i].astype(F32)).astype(BF16)
    gq_store = pltpu.make_async_copy(gq_all, gq_ref, local_sem.at[9])
    gq_store.start()
    for kind in (GV, GK):
        y_arrived(kind)
    for kind in (GV, GK, GQ):
        y_drain(kind)
    for store in own_stores:
        store.wait()
    gw_store.wait()
    gq_store.wait()


def deliver(*refs):
    count = (len(refs) - 1) // 3
    sources, results, stages = (refs[i * count : (i + 1) * count] for i in range(3))
    sem = refs[-1]
    fetches = [
        pltpu.make_async_copy(sources[i], stages[i], sem.at[0, i]) for i in range(count)
    ]
    stores = [
        pltpu.make_async_copy(stages[i], results[i], sem.at[1, i]) for i in range(count)
    ]
    for fetch in fetches:
        fetch.start()
    for fetch, store in zip(fetches, stores):
        fetch.wait()
        store.start()
    for store in stores:
        store.wait()


def on_device(
    queries, key_vectors, value_vectors, saved_out, grad_out, out_weight, window_start, block_order
):
    vmem = pl.BlockSpec(memory_space=pltpu.VMEM)
    smem = pl.BlockSpec(memory_space=pltpu.SMEM)
    hbm = pl.BlockSpec(memory_space=pl.ANY)

    def buf(*shape, dtype=BF16):
        return pltpu.VMEM(shape, dtype)

    dma = pltpu.SemaphoreType.DMA
    rows = (HEADS, WINDOW)
    scratch = [
        buf(Q_ROWS, WIDTH), buf(Q_ROWS, WIDTH), buf(Q_ROWS, WIDTH),
        buf(NY, K_ROWS, COLS), buf(NY, K_ROWS, COLS),
        buf(NZ, GROUP, COLS), buf(NZ, SLOT, HD), buf(NZ, W_ROWS, W_COLS),
        buf(ND, GROUP, COLS), buf(ND, GROUP, W_COLS),
        buf(NY, 2 * Q_ROWS, HALF), buf(NY, 2 * Q_ROWS, HALF),
        buf(NY, 2 * Q_ROWS, HALF), buf(NY, 2 * Q_ROWS, HALF),
        buf(2 * Q_ROWS, WIDTH // 2), buf(NY, 2 * Q_ROWS, WIDTH // 2),
        buf(ND, GROUP, W_COLS),
        buf(CHUNKS, ND, GROUP, CHUNK), buf(CHUNKS, ND, GROUP, CHUNK),
        buf(HEADS, KEYS, WINDOW),
        buf(8, WINDOW, dtype=F32),
        buf(*rows, dtype=F32), buf(*rows, dtype=F32), buf(*rows, dtype=F32),
        buf(3, *rows, dtype=F32), buf(3, *rows, dtype=F32),
        buf(*rows, dtype=F32), buf(*rows, dtype=F32),
        buf(NY, K_ROWS, COLS), buf(NY, K_ROWS, COLS),
        buf(NZ, GROUP, COLS, dtype=F32), buf(NZ, W_ROWS, W_COLS, dtype=F32),
        buf(W_ROWS, W_COLS, dtype=F32),
        buf(16, GROUP, COLS), buf(16, GROUP, COLS),
        buf(HALF_Z, W_ROWS, W_COLS), buf(HALF_Z, W_ROWS, W_COLS),
        buf(HALF_Z, W_ROWS, W_COLS), buf(HALF_Z, W_ROWS, W_COLS),
        buf(NY, 2 * Q_ROWS, HALF), buf(NY, 2 * Q_ROWS, HALF),
        buf(Q_ROWS, WIDTH),
        dma((8, NY - 1)), dma((8, NY)),
        dma((2 + CHUNKS, ND - 1)), dma((2 + CHUNKS, ND)),
        dma((3, NZ)), dma((3, NZ)),
        dma((6,)), dma((6,)),
        dma((16,)), dma((16,)),
        dma((NZ,)), dma((NZ,)),
        dma((10,)),
    ]
    shapes = (
        jax.ShapeDtypeStruct((Q_ROWS, WIDTH), BF16),
        jax.ShapeDtypeStruct((K_ROWS, WIDTH), BF16),
        jax.ShapeDtypeStruct((K_ROWS, WIDTH), BF16),
        jax.ShapeDtypeStruct((W_ROWS, W_COLS), F32),
    )
    outs = pl.pallas_call(
        kernel,
        out_shape=shapes,
        in_specs=[pl.BlockSpec(memory_space=pltpu.HBM)] * 6 + [vmem, smem],
        out_specs=(hbm,) * 4,
        scratch_shapes=scratch,
        compiler_params=pltpu.CompilerParams(
            collective_id=0, has_side_effects=True, vmem_limit_bytes=VMEM_BYTES
        ),
        name="attention_backward",
    )(
        queries[0], saved_out[0], grad_out[0], key_vectors[0], value_vectors[0], out_weight,
        block_order.reshape(1, NY * NZ), window_start,
    )
    outs = pl.pallas_call(
        deliver,
        out_shape=shapes,
        in_specs=[hbm] * 4,
        out_specs=(hbm,) * 4,
        scratch_shapes=[pltpu.VMEM(shape.shape, shape.dtype) for shape in shapes] + [dma((2, 4))],
        compiler_params=pltpu.CompilerParams(vmem_limit_bytes=VMEM_BYTES),
        name="deliver",
    )(*outs)
    return (outs[0][None], outs[1][None], outs[2][None], outs[3])


def solution(mesh):
    rows = P("dp", "seq", None)
    return jax.shard_map(
        on_device,
        mesh=mesh,
        in_specs=(rows, rows, rows, rows, rows, P("seq", "dp"), P("dp"), P()),
        out_specs=(rows, rows, rows, P("seq", "dp")),
        check_vma=False,
    )
```

time: 155 us -> 124 us (0.80)
  Pallas kernels: 144 us -> 123 us
  local copies, waits for them, and re-layouts: 8.55 us -> 0 us
    pallas_call x1 -> x2, Pallas kernels: 144 us -> 123 us  [the longest x1 120 us: on_device(): pl.pallas_call(kernel, out_shape=shapes, in_specs=[pl.BlockSpec(memory_sp...]
    unnamed x16 -> x0, local copies, waits for them, and re-layouts: 8.19 us -> none
where the time goes in v2:
time: 124 us
  Pallas kernels  123 us (99%)
  between operations  1.29 us (1%)
    pallas_call x1, Pallas kernels, on_device(): pl.pallas_call(kernel, out_shape=shapes, in_specs=[pl.BlockSpec(memory_sp...  120 us
    pallas_call x1, Pallas kernels, on_device(): pl.pallas_call(deliver, out_shape=shapes, in_specs=[hbm] * 4, out_specs=(...  2.68 us

profile of v2, /device:TPU:24, one launch (start us, length us, event | category | flops | bytes accessed | tf_op | source)
XLA Modules:
  0.0 124.0 jit_solution(7235955191609585016)
XLA Ops:
  1.3 120.0 %attention_backward.1 = (bf16[8,4096]{1,0:T(8,128)(2,1)}, bf16[128,4096]{1,0:T(8,128)(2,1)}, bf16[128,4096]{1,0:T(8,128)(2,1)}, f32[64,512]{1,0:T(8,128)}) custom-call(bf16[8,4096]{1,0:T(8,128)(2,1)} %bitcast.11, bf16[8,4096]{1,0:T(8,128)(2,1)} %bitcast.12, bf16[8,4096]{1,0:T(8,128)(2,1)} %bitcast.13, bf16[128,4096]{1,0:T(8,128)(2,1)} %bitcast.9, ...), custom_call_target="tpu_custom_call" | custom-call | tf_op jit(solution)/shard_map/attention_backward/pallas_call | solution.py:627
  121.3 2.7 %deliver.1 = (bf16[8,4096]{1,0:T(8,128)(2,1)}, bf16[128,4096]{1,0:T(8,128)(2,1)}, bf16[128,4096]{1,0:T(8,128)(2,1)}, f32[64,512]{1,0:T(8,128)}) custom-call(bf16[8,4096]{1,0:T(8,128)(2,1)} %get-tuple-element.12.refs_0_, bf16[128,4096]{1,0:T(8,128)(2,1)} %get-tuple-element.13.refs_1_, bf16[128,4096]{1,0:T(8,128)(2,1)} %get-tuple-element.14.refs_2_, ...), custom_call_target="tpu_custom_call" | custom-call | tf_op jit(solution)/shard_map/deliver/pallas_call | solution.py:641

commit v3 on v2

--- a/solution.py
+++ b/solution.py
@@ -27,7 +27,9 @@
 CHUNKS = 4
 CHUNK = COLS // CHUNKS
 BLOCK = WINDOW // CHUNKS
-SLOT = HEADS * GROUP + 2 * HEADS
+PARTS = 2
+PART_HEADS = HEADS // PARTS
+SLOT = PART_HEADS * GROUP + 16
 NEAR = 4
 JUMP = 5
 VMEM_BYTES = 64 * 1024 * 1024
@@ -158,7 +160,7 @@
             device_id=device, device_id_type=MESH,
         )
 
-    streams = [wg, qg, cg]
+    streams = [wg, qg, cg.at[0], cg.at[1]]
 
     def z_send(stream, sem, distance, hop):
         buf, slot = streams[stream], z_off(-distance)
@@ -213,7 +215,10 @@
         def _(sem):
             z_send(stream, sem, 0, 1).wait_send()
 
-    W, Q, C = 0, 1, 2
+    W, Q, C = 0, 1, (2, 3)
+
+    def part_cols(p, part):
+        return pl.ds(pl.multiple_of(p * COLS + part * HALF, HALF), HALF)
 
     kinds = [
         (lambda p: go_out, lambda p: go_in.at[p]),
@@ -221,11 +226,14 @@
         (lambda p: so_out.at[p], lambda p: so_in.at[p]),
         (lambda p: k_ref.at[:, cols_of(p)], lambda p: kb.at[p]),
         (lambda p: v_ref.at[:, cols_of(p)], lambda p: vb.at[p]),
-        (lambda p: gvs.at[p], lambda p: gv_ref.at[:, cols_of(p)]),
-        (lambda p: gks.at[p], lambda p: gk_ref.at[:, cols_of(p)]),
-        (lambda p: gq_out.at[p], lambda p: gq_in.at[p]),
+        (lambda p: gvs.at[0, p], lambda p: gv_ref.at[:, part_cols(p, 0)]),
+        (lambda p: gvs.at[1, p], lambda p: gv_ref.at[:, part_cols(p, 1)]),
+        (lambda p: gks.at[0, p], lambda p: gk_ref.at[:, part_cols(p, 0)]),
+        (lambda p: gks.at[1, p], lambda p: gk_ref.at[:, part_cols(p, 1)]),
+        (lambda p: gq_out.at[0, p], lambda p: gq_in.at[0, p]),
+        (lambda p: gq_out.at[1, p], lambda p: gq_in.at[1, p]),
     ]
-    GV, GK, GQ = 5, 6, 7
+    GV, GK, GQ = (5, 6), (7, 8), (9, 10)
 
     def y_copy(kind, j, slot):
         src_of, dst_of = kinds[kind]
@@ -358,21 +366,60 @@
         lse = joined(lse_near[...], [lse_b[j] for j in range(3)])
         scale[...] = jnp.exp2(row_max[...] - lse)
 
-    def both(k):
-        ring_step(W, k)
-        ring_step(Q, k)
-
+    lane = lax.broadcasted_iota(jnp.int32, (GROUP, HD), 1)
+    lane_head = (lane & 3) + ((lane >> 3) & 1) * PART_HEADS
+
+    def own_context(i, sums):
+        d_arrived(2 + i, c_in.at[i])
+        context = c_in[i, 0].astype(F32)
+        for d in range(1, ND):
+            context = context + c_in[i, d].astype(F32)
+        context = context.astype(BF16)
+        chunk = nth_block(i)
+        lanes = pl.ds(pl.multiple_of(chunk * CHUNK, CHUNK), CHUNK)
+        product = context.astype(F32) * sog[pl.ds(s, 1), :, lanes][0].astype(F32)
+        part = pl.ds(lax.div(chunk, 2), 1)
+        for j in range(CHUNK // HD):
+            first = lax.rem(chunk, 2) * (CHUNK // HD * GROUP) + j * GROUP
+            own = slice(j * HD, (j + 1) * HD)
+            cg[part, pl.ds(z, 1), pl.ds(pl.multiple_of(first, GROUP), GROUP), :] = context[
+                :, own
+            ][None, None]
+            one = jnp.sum(product[:, own], 1, keepdims=True)
+            sums = jnp.where(lane_head == chunk * (CHUNK // HD) + j, one, sums)
+        return sums
+
+    def own_delta(sums):
+        high = sums.astype(BF16).astype(F32)
+        rest = jnp.where((lane & PART_HEADS) == 0, high, sums - high).astype(BF16)
+        row = lax.broadcasted_iota(jnp.int32, (GROUP, HD), 0)
+        place = jnp.where(lane == row + z_low * GROUP, 1.0, 0.0).astype(BF16)
+        tiles = dot_tn(rest, place)
+        for p in range(PARTS):
+            tile = tiles[8 * p : 8 * p + 8]
+            tile = jnp.concatenate([tile, jnp.zeros_like(tile)], 0)
+            cg[p, pl.ds(z, 1), PART_HEADS * GROUP :, :] = tile.astype(BF16)[None]
+
+    def halves(k):
+        ring_step(C[0], k)
+        ring_step(C[1], k)
+
+    def projection_gradient(i):
+        block = sog[:, :, i * CHUNK : (i + 1) * CHUNK].reshape(ND * GROUP, CHUNK)
+        piece = dot_tn(block, gg[...].reshape(ND * GROUP, W_COLS))
+        gwp[4 * i : 4 * i + 4] = piece.reshape(4, W_ROWS, W_COLS)
+
+    ring_start(W)
     y_start(1)
     y_start(0)
-    ring_start(W)
-    for kind in range(2, 5):
-        y_start(kind)
-
+    y_start(2)
+
+    ring_step(W, 1)
     y_arrived(1)
     rows = [unfold(q_in[i].astype(F32)) for i in range(NY)]
     qg[pl.ds(z, 1)] = jnp.concatenate(rows, 0).astype(BF16)[None]
     ring_start(Q)
-
+    ring_step(W, 2)
     y_arrived(0)
     for d in range(ND):
         top, off = d // (ND // 2), (d % (ND // 2)) * W_COLS
@@ -383,31 +430,47 @@
         g_out[d] = jnp.concatenate(piece, 0).astype(BF16)
     gg[pl.ds(s, 1)] = g_out[pl.ds(s, 1)]
     d_start(0, lambda p: g_out.at[p], gg)
-
-    both(1)
+    ring_step(Q, 1)
+    ring_step(W, 3)
     y_arrived(2)
     rows = [unfold(so_in[i].astype(F32)) for i in range(NY)]
     sog[pl.ds(s, 1)] = jnp.concatenate(rows, 0).astype(BF16)[None]
     d_start(1, lambda p: sog.at[s], sog)
 
-    both(2)
-    both(3)
+    y_start(3)
+    y_start(4)
+    ring_step(Q, 2)
+    ring_step(W, 4)
+    ring_step(Q, 3)
+    ring_step(W, 5)
     d_arrived(0, gg)
+    d_arrived(1, sog)
+    projection_gradient(0)
+    projection_gradient(1)
     partial_context(0)
-    both(4)
-    both(5)
+    ring_step(Q, 4)
+    ring_step(W, 6)
+    projection_gradient(2)
+    projection_gradient(3)
+    gw_step(0)
     partial_context(1)
-    both(6)
-    d_arrived(1, sog)
-    for i in range(CHUNKS):
-        block = sog[:, :, i * CHUNK : (i + 1) * CHUNK].reshape(ND * GROUP, CHUNK)
-        piece = dot_tn(block, gg[...].reshape(ND * GROUP, W_COLS))
-        gwp[4 * i : 4 * i + 4] = piece.reshape(4, W_ROWS, W_COLS)
-    both(7)
+    ring_step(Q, 5)
+    ring_step(W, 7)
+    gw_step(1)
     partial_context(2)
+    ring_step(Q, 6)
     ring_step(W, 8)
     partial_context(3)
-    ring_step(Q, 8)
+    sums = jnp.zeros((GROUP, HD), F32)
+    for i in range(3):
+        sums = own_context(i, sums)
+    ring_step(Q, 7)
+    gw_step(2)
+    sums = own_context(3, sums)
+    own_delta(sums)
+    ring_start(C[0])
+    ring_start(C[1])
+    ring_step(Q, HALF_Z)
 
     loads[4].wait()
     y_arrived(3)
@@ -416,139 +479,139 @@
     def _(h):
         softmax_head(h)
 
+        @pl.when(h == PART_HEADS - 1)
+        def _():
+            halves(1)
+
     lse_start()
-
-    lane = lax.broadcasted_iota(jnp.int32, (GROUP, HD), 1)
-    sums = jnp.zeros((GROUP, HD), F32)
-    for i in range(CHUNKS):
-        d_arrived(2 + i, c_in.at[i])
-        context = c_in[i, 0].astype(F32)
-        for d in range(1, ND):
-            context = context + c_in[i, d].astype(F32)
-        context = context.astype(BF16)
-        chunk = nth_block(i)
-        lanes = pl.ds(pl.multiple_of(chunk * CHUNK, CHUNK), CHUNK)
-        product = context.astype(F32) * sog[pl.ds(s, 1), :, lanes][0].astype(F32)
-        for j in range(CHUNK // HD):
-            h = chunk * (CHUNK // HD) + j
-            own = slice(j * HD, (j + 1) * HD)
-            cg[pl.ds(z, 1), pl.ds(pl.multiple_of(h * GROUP, GROUP), GROUP), :] = context[:, own][None]
-            one = jnp.sum(product[:, own], 1, keepdims=True)
-            sums = jnp.where((lane & (HEADS - 1)) == h, one, sums)
-    high = sums.astype(BF16).astype(F32)
-    rest = jnp.where(lane < HEADS, high, sums - high).astype(BF16)
-    row = lax.broadcasted_iota(jnp.int32, (GROUP, HD), 0)
-    place = jnp.where(lane == row + z_low * GROUP, 1.0, 0.0).astype(BF16)
-    cg[pl.ds(z, 1), HEADS * GROUP :, :] = dot_tn(rest, place)[: 2 * HEADS].astype(BF16)[None]
-    wave_start(C)
-    wave_near(C, 1)
+    halves(2)
+    gw_step(3)
+    halves(3)
     lse_next()
-    wave_near(C, 2)
-    gw_step(0)
-    wave_far(C, 1)
-    wave_near(C, 3)
-    gw_step(1)
-    wave_far(C, 2)
+    halves(4)
+    gw_step(4)
+    halves(5)
+    halves(6)
+    gw_step(5)
+    halves(7)
     lse_end()
-    wave_near(C, 4)
-    gw_step(2)
-    wave_far(C, 3)
-    gw_step(3)
-    wave_far(C, 4)
     loads[5].wait()
     y_arrived(4)
+    ring_step(C[0], 8)
 
     chains = [(1, HALF_Z, 4), (-1, HALF_Z - 1, 3), (1, NEAR, 4), (-1, NEAR, 4)]
 
-    def dq_copy(c, k):
+    def dq_copy(part, c, k):
         sign, reach, length = chains[c]
         hop = sign * JUMP if reach > NEAR and k == length - 1 else sign
         i = 4 * c + k
-        return remote(dq_send.at[i], dq_recv.at[i], dq_ssem.at[i], dq_rsem.at[i], at_z(hop))
-
-    def dq_step(k):
+        return remote(
+            dq_send.at[part, i], dq_recv.at[part, i], dq_ssem.at[part, i], dq_rsem.at[part, i],
+            at_z(hop),
+        )
+
+    def dq_step(part, k):
         for c, (sign, reach, length) in enumerate(chains):
             if k < length:
-                mine = dq[pl.ds(z_off(sign * (reach - k)), 1)][0]
+                mine = dq[part, pl.ds(z_off(sign * (reach - k)), 1)][0]
                 if k > 0:
-                    dq_copy(c, k - 1).wait_recv()
-                    mine = mine + dq_recv[4 * c + k - 1].astype(F32)
-                dq_send[4 * c + k] = mine.astype(BF16)
-                dq_copy(c, k).start()
-
-    def dq_end():
-        total = dq[pl.ds(z, 1)][0]
+                    dq_copy(part, c, k - 1).wait_recv()
+                    mine = mine + dq_recv[part, 4 * c + k - 1].astype(F32)
+                dq_send[part, 4 * c + k] = mine.astype(BF16)
+                dq_copy(part, c, k).start()
+
+    def dq_end(part):
+        total = dq[part, pl.ds(z, 1)][0]
         for c in (2, 3, 0, 1):
             last = chains[c][2] - 1
-            dq_copy(c, last).wait_recv()
-            total = total + dq_recv[4 * c + last].astype(F32)
+            dq_copy(part, c, last).wait_recv()
+            total = total + dq_recv[part, 4 * c + last].astype(F32)
         total = total * INV_ROOT
         for i in range(NY):
-            gq_out[i] = fold(total[i * Q_ROWS : (i + 1) * Q_ROWS]).astype(BF16)
-        gq_in[pl.ds(y, 1)] = gq_out[pl.ds(y, 1)]
-        y_start(GQ)
-
-    for i in range(CHUNKS):
-        tile = cg[4 * i : 4 * i + 4, HEADS * GROUP :, :].astype(F32)
-        tile = tile[0] + tile[1] + tile[2] + tile[3]
-        delta[:, i * BLOCK : (i + 1) * BLOCK] = tile[:HEADS] + tile[HEADS:]
-
-    @pl.loop(0, HEADS, unroll=2)
-    def _(h):
-        lanes = pl.ds(pl.multiple_of(h * HD, HD), HD)
-        query = qg[:, :, lanes].reshape(WINDOW, HD)
-        head_rows = pl.ds(pl.multiple_of(h * GROUP, GROUP), GROUP)
-        ctx = cg[:, head_rows, :].reshape(WINDOW, HD)
-        attend = prob[h].astype(F32) * scale[pl.ds(h, 1), :]
-        value_grad = dot_nn(attend.astype(BF16), ctx)
-        dprob = dot_nt(vb[:, :, lanes].reshape(KEYS, HD), ctx)
-        dscore = (attend * (dprob - delta[pl.ds(h, 1), :])).astype(BF16)
-        key_grad = dot_nn(dscore, query) * INV_ROOT
-        query_grad = dot_tn(dscore, kb[:, :, lanes].reshape(KEYS, HD))
-        gvs[:, :, lanes] = value_grad.astype(BF16).reshape(NY, K_ROWS, HD)
-        gks[:, :, lanes] = key_grad.astype(BF16).reshape(NY, K_ROWS, HD)
-        dq[:, :, lanes] = query_grad.reshape(NZ, GROUP, HD)
-
-    dq_step(0)
-    y_start(GV)
-    y_start(GK)
+            gq_out[part, i] = fold(total[i * Q_ROWS : (i + 1) * Q_ROWS]).astype(BF16)
+        gq_in[part, pl.ds(y, 1)] = gq_out[part, pl.ds(y, 1)]
+        y_start(GQ[part])
+
     own_stores = [
-        pltpu.make_async_copy(src.at[y], dst.at[:, cols_of(y)], local_sem.at[7 + i])
+        pltpu.make_async_copy(
+            src.at[part, y], dst.at[:, part_cols(y, part)], local_sem.at[7 + 2 * part + i]
+        )
+        for part in range(PARTS)
         for i, (src, dst) in enumerate([(gvs, gv_ref), (gks, gk_ref)])
     ]
-    for store in own_stores:
-        store.start()
-    dq_step(1)
-    gw_step(4)
+
+    def gradients(part):
+        for i in range(CHUNKS):
+            tile = cg[part, 4 * i : 4 * i + 4, PART_HEADS * GROUP :, :].astype(F32)
+            tile = tile[0] + tile[1] + tile[2] + tile[3]
+            delta[part, :PART_HEADS, i * BLOCK : (i + 1) * BLOCK] = (
+                tile[:PART_HEADS] + tile[PART_HEADS : 2 * PART_HEADS]
+            )
+
+        @pl.loop(0, PART_HEADS, unroll=2)
+        def _(i):
+            h = part * PART_HEADS + i
+            own = pl.ds(pl.multiple_of(i * HD, HD), HD)
+            lanes = pl.ds(pl.multiple_of(h * HD, HD), HD)
+            query = qg[:, :, lanes].reshape(WINDOW, HD)
+            head_rows = pl.ds(pl.multiple_of(i * GROUP, GROUP), GROUP)
+            ctx = cg[part, :, head_rows, :].reshape(WINDOW, HD)
+            attend = prob[h].astype(F32) * scale[pl.ds(h, 1), :]
+            value_grad = dot_nn(attend.astype(BF16), ctx)
+            dprob = dot_nt(vb[:, :, lanes].reshape(KEYS, HD), ctx)
+            dscore = (attend * (dprob - delta[part, pl.ds(i, 1), :])).astype(BF16)
+            key_grad = dot_nn(dscore, query) * INV_ROOT
+            query_grad = dot_tn(dscore, kb[:, :, lanes].reshape(KEYS, HD))
+            gvs[part, :, :, own] = value_grad.astype(BF16).reshape(NY, K_ROWS, HD)
+            gks[part, :, :, own] = key_grad.astype(BF16).reshape(NY, K_ROWS, HD)
+            dq[part, :, :, own] = query_grad.reshape(NZ, GROUP, HD)
+
+        dq_step(part, 0)
+        y_start(GV[part])
+        y_start(GK[part])
+        own_stores[2 * part].start()
+        own_stores[2 * part + 1].start()
+
+    gradients(0)
+    gw_step(6)
+    ring_step(C[1], 8)
+    gradients(1)
+    gw_step(7)
+    dq_step(0, 1)
     z_drain(W)
+    dq_step(1, 1)
     z_drain(Q)
-    dq_step(2)
-    gw_step(5)
-    z_drain(C)
-    dq_step(3)
-    gw_step(6)
+    dq_step(0, 2)
+    dq_step(1, 2)
+    z_drain(C[0])
+    z_drain(C[1])
+    dq_step(0, 3)
+    dq_step(1, 3)
     for copy in d_sends:
         copy.wait_send()
     for kind in range(5):
         y_drain(kind)
-    gw_step(7)
-    dq_end()
+    dq_end(0)
+    dq_end(1)
     gw_end()
     for k in range(HALF_Z):
         gw_right(k).wait_send()
     for k in range(HALF_Z - 1):
         gw_left(k).wait_send()
-    for c, (_, _, length) in enumerate(chains):
-        for k in range(length):
-            dq_copy(c, k).wait_send()
-    y_arrived(GQ)
-    for i in range(NY):
-        gq_all[:, i * COLS : (i + 1) * COLS] = unfold(gq_in[i].astype(F32)).astype(BF16)
-    gq_store = pltpu.make_async_copy(gq_all, gq_ref, local_sem.at[9])
+    for part in range(PARTS):
+        for c, (_, _, length) in enumerate(chains):
+            for k in range(length):
+                dq_copy(part, c, k).wait_send()
+    for part in range(PARTS):
+        y_arrived(GQ[part])
+        for i in range(NY):
+            first = i * COLS + part * HALF
+            gq_all[:, first : first + HALF] = unfold(gq_in[part, i].astype(F32)).astype(BF16)
+    gq_store = pltpu.make_async_copy(gq_all, gq_ref, local_sem.at[11])
     gq_store.start()
-    for kind in (GV, GK):
+    for kind in GV + GK:
         y_arrived(kind)
-    for kind in (GV, GK, GQ):
+    for kind in GV + GK + GQ:
         y_drain(kind)
     for store in own_stores:
         store.wait()
@@ -590,7 +653,7 @@
     scratch = [
         buf(Q_ROWS, WIDTH), buf(Q_ROWS, WIDTH), buf(Q_ROWS, WIDTH),
         buf(NY, K_ROWS, COLS), buf(NY, K_ROWS, COLS),
-        buf(NZ, GROUP, COLS), buf(NZ, SLOT, HD), buf(NZ, W_ROWS, W_COLS),
+        buf(NZ, GROUP, COLS), buf(PARTS, NZ, SLOT, HD), buf(NZ, W_ROWS, W_COLS),
         buf(ND, GROUP, COLS), buf(ND, GROUP, W_COLS),
         buf(NY, 2 * Q_ROWS, HALF), buf(NY, 2 * Q_ROWS, HALF),
         buf(NY, 2 * Q_ROWS, HALF), buf(NY, 2 * Q_ROWS, HALF),
@@ -601,22 +664,22 @@
         buf(8, WINDOW, dtype=F32),
         buf(*rows, dtype=F32), buf(*rows, dtype=F32), buf(*rows, dtype=F32),
         buf(3, *rows, dtype=F32), buf(3, *rows, dtype=F32),
-        buf(*rows, dtype=F32), buf(*rows, dtype=F32),
-        buf(NY, K_ROWS, COLS), buf(NY, K_ROWS, COLS),
-        buf(NZ, GROUP, COLS, dtype=F32), buf(NZ, W_ROWS, W_COLS, dtype=F32),
+        buf(*rows, dtype=F32), buf(PARTS, 8, WINDOW, dtype=F32),
+        buf(PARTS, NY, K_ROWS, HALF), buf(PARTS, NY, K_ROWS, HALF),
+        buf(PARTS, NZ, GROUP, HALF, dtype=F32), buf(NZ, W_ROWS, W_COLS, dtype=F32),
         buf(W_ROWS, W_COLS, dtype=F32),
-        buf(16, GROUP, COLS), buf(16, GROUP, COLS),
+        buf(PARTS, 16, GROUP, HALF), buf(PARTS, 16, GROUP, HALF),
         buf(HALF_Z, W_ROWS, W_COLS), buf(HALF_Z, W_ROWS, W_COLS),
         buf(HALF_Z, W_ROWS, W_COLS), buf(HALF_Z, W_ROWS, W_COLS),
-        buf(NY, 2 * Q_ROWS, HALF), buf(NY, 2 * Q_ROWS, HALF),
+        buf(PARTS, NY, 2 * Q_ROWS, HALF // 2), buf(PARTS, NY, 2 * Q_ROWS, HALF // 2),
         buf(Q_ROWS, WIDTH),
-        dma((8, NY - 1)), dma((8, NY)),
+        dma((11, NY - 1)), dma((11, NY)),
         dma((2 + CHUNKS, ND - 1)), dma((2 + CHUNKS, ND)),
-        dma((3, NZ)), dma((3, NZ)),
+        dma((4, NZ)), dma((4, NZ)),
         dma((6,)), dma((6,)),
-        dma((16,)), dma((16,)),
+        dma((PARTS, 16)), dma((PARTS, 16)),
         dma((NZ,)), dma((NZ,)),
-        dma((10,)),
+        dma((12,)),
     ]
     shapes = (
         jax.ShapeDtypeStruct((Q_ROWS, WIDTH), BF16),

time: 124 us -> 117 us (0.944)
  Pallas kernels: 123 us -> 115 us
    pallas_call x1, Pallas kernels: 120 us -> 112 us  [on_device(): pl.pallas_call(kernel, out_shape=shapes, in_specs=[pl.BlockSpec(memory_sp...]
where the time goes in v3:
time: 117 us; the launch traced here: 116 us
  Pallas kernels  115 us (98%)
  between operations  1.29 us (1%)
    pallas_call x1, Pallas kernels, on_device(): pl.pallas_call(kernel, out_shape=shapes, in_specs=[pl.BlockSpec(memory_sp...  112 us
    pallas_call x1, Pallas kernels, on_device(): pl.pallas_call(deliver, out_shape=shapes, in_specs=[hbm] * 4, out_specs=(...  2.68 us

profile of v3, /device:TPU:24, one launch (start us, length us, event | category | flops | bytes accessed | tf_op | source)
XLA Modules:
  0.0 116.1 jit_solution(14325015598205176558)
XLA Ops:
  1.3 112.2 %attention_backward.1 = (bf16[8,4096]{1,0:T(8,128)(2,1)}, bf16[128,4096]{1,0:T(8,128)(2,1)}, bf16[128,4096]{1,0:T(8,128)(2,1)}, f32[64,512]{1,0:T(8,128)}) custom-call(bf16[8,4096]{1,0:T(8,128)(2,1)} %bitcast.11, bf16[8,4096]{1,0:T(8,128)(2,1)} %bitcast.12, bf16[8,4096]{1,0:T(8,128)(2,1)} %bitcast.13, bf16[128,4096]{1,0:T(8,128)(2,1)} %bitcast.9, ...), custom_call_target="tpu_custom_call" | custom-call | tf_op jit(solution)/shard_map/attention_backward/pallas_call | solution.py:690
  113.4 2.7 %deliver.1 = (bf16[8,4096]{1,0:T(8,128)(2,1)}, bf16[128,4096]{1,0:T(8,128)(2,1)}, bf16[128,4096]{1,0:T(8,128)(2,1)}, f32[64,512]{1,0:T(8,128)}) custom-call(bf16[8,4096]{1,0:T(8,128)(2,1)} %get-tuple-element.12.refs_0_, bf16[128,4096]{1,0:T(8,128)(2,1)} %get-tuple-element.13.refs_1_, bf16[128,4096]{1,0:T(8,128)(2,1)} %get-tuple-element.14.refs_2_, ...), custom_call_target="tpu_custom_call" | custom-call | tf_op jit(solution)/shard_map/deliver/pallas_call | solution.py:704

commit v4 on v3

--- a/solution.py
+++ b/solution.py
@@ -66,7 +66,7 @@
     q_own, so_own, go_own,
     kb, vb, qg, cg, wg, sog, gg,
     q_out, q_in, so_out, so_in, go_out, go_in, g_out,
-    c_out, c_in, prob, query_pos, row_max, lse_own, lse_near, lse_a, lse_b, scale, delta,
+    c_out, c_in, prob, query_pos, row_max, lse_own, lse_near, lse_a, lse_b, lse_all, scale, delta,
     gvs, gks, dq, gwp, gw_out,
     dq_send, dq_recv, gw_sr, gw_sl, gw_rr, gw_rl, gq_out, gq_in, gq_all,
     y_send, y_recv, d_send, d_recv, ag_send, ag_recv, l_send, l_recv,
@@ -335,10 +335,20 @@
         row_max[pl.ds(h, 1), :] = top
         lse_own[pl.ds(h, 1), :] = top + jnp.log2(total)
 
+    def lane_block(i):
+        return pl.ds(pl.multiple_of(i * BLOCK, BLOCK), BLOCK)
+
     def lse_copy(level, j):
-        src, dst = ((lse_own, lse_a), (lse_near, lse_b))[level]
+        low = lax.rem(z_low + j + 1, 4)
+        src, dst = (
+            (lse_own.at[:, lane_block(low)], lse_a.at[j]),
+            (lse_near, lse_b.at[j]),
+            (lse_all.at[z_low], lse_all.at[z_low]),
+        )[level]
         i = level * 3 + j
-        return remote(src, dst.at[j], l_send.at[i], l_recv.at[i], (near, far)[level][j])
+        return remote(
+            src, dst, l_send.at[i], l_recv.at[i], (near, far, near)[level][j]
+        )
 
     def joined(first, others):
         most = first
@@ -356,14 +366,21 @@
     def lse_next():
         for j in range(3):
             lse_copy(0, j).wait()
-        lse_near[...] = joined(lse_own[...], [lse_a[j] for j in range(3)])
+        lse_near[...] = joined(lse_own[:, lane_block(z_low)], [lse_a[j] for j in range(3)])
         for j in range(3):
             lse_copy(1, j).start()
 
+    def lse_last():
+        for j in range(3):
+            lse_copy(1, j).wait()
+        lse_all[pl.ds(z_low, 1)] = joined(lse_near[...], [lse_b[j] for j in range(3)])[None]
+        for j in range(3):
+            lse_copy(2, j).start()
+
     def lse_end():
         for j in range(3):
-            lse_copy(1, j).wait()
-        lse = joined(lse_near[...], [lse_b[j] for j in range(3)])
+            lse_copy(2, j).wait()
+        lse = jnp.concatenate([lse_all[i] for i in range(4)], 1)
         scale[...] = jnp.exp2(row_max[...] - lse)
 
     lane = lax.broadcasted_iota(jnp.int32, (GROUP, HD), 1)
@@ -479,18 +496,20 @@
     def _(h):
         softmax_head(h)
 
-        @pl.when(h == PART_HEADS - 1)
-        def _():
-            halves(1)
+        for k in (1, 2):
+
+            @pl.when(h == PART_HEADS * k - 3)
+            def _():
+                halves(k)
 
     lse_start()
-    halves(2)
     gw_step(3)
     halves(3)
     lse_next()
     halves(4)
     gw_step(4)
     halves(5)
+    lse_last()
     halves(6)
     gw_step(5)
     halves(7)
@@ -548,7 +567,7 @@
                 tile[:PART_HEADS] + tile[PART_HEADS : 2 * PART_HEADS]
             )
 
-        @pl.loop(0, PART_HEADS, unroll=2)
+        @pl.loop(0, PART_HEADS, unroll=4)
         def _(i):
             h = part * PART_HEADS + i
             own = pl.ds(pl.multiple_of(i * HD, HD), HD)
@@ -621,14 +640,20 @@
 
 def deliver(*refs):
     count = (len(refs) - 1) // 3
-    sources, results, stages = (refs[i * count : (i + 1) * count] for i in range(3))
     sem = refs[-1]
-    fetches = [
-        pltpu.make_async_copy(sources[i], stages[i], sem.at[0, i]) for i in range(count)
-    ]
-    stores = [
-        pltpu.make_async_copy(stages[i], results[i], sem.at[1, i]) for i in range(count)
-    ]
+    fetches, stores = [], []
+    for source, result, stage in zip(*(refs[i * count : (i + 1) * count] for i in range(3))):
+        rows = source.shape[0]
+        size = min(rows, 32)
+        for first in range(0, rows, size):
+            piece = pl.ds(first, size)
+            n = len(fetches)
+            fetches.append(
+                pltpu.make_async_copy(source.at[piece], stage.at[piece], sem.at[0, n])
+            )
+            stores.append(
+                pltpu.make_async_copy(stage.at[piece], result.at[piece], sem.at[1, n])
+            )
     for fetch in fetches:
         fetch.start()
     for fetch, store in zip(fetches, stores):
@@ -662,8 +687,9 @@
         buf(CHUNKS, ND, GROUP, CHUNK), buf(CHUNKS, ND, GROUP, CHUNK),
         buf(HEADS, KEYS, WINDOW),
         buf(8, WINDOW, dtype=F32),
-        buf(*rows, dtype=F32), buf(*rows, dtype=F32), buf(*rows, dtype=F32),
-        buf(3, *rows, dtype=F32), buf(3, *rows, dtype=F32),
+        buf(*rows, dtype=F32), buf(*rows, dtype=F32), buf(HEADS, BLOCK, dtype=F32),
+        buf(3, HEADS, BLOCK, dtype=F32), buf(3, HEADS, BLOCK, dtype=F32),
+        buf(4, HEADS, BLOCK, dtype=F32),
         buf(*rows, dtype=F32), buf(PARTS, 8, WINDOW, dtype=F32),
         buf(PARTS, NY, K_ROWS, HALF), buf(PARTS, NY, K_ROWS, HALF),
         buf(PARTS, NZ, GROUP, HALF, dtype=F32), buf(NZ, W_ROWS, W_COLS, dtype=F32),
@@ -676,7 +702,7 @@
         dma((11, NY - 1)), dma((11, NY)),
         dma((2 + CHUNKS, ND - 1)), dma((2 + CHUNKS, ND)),
         dma((4, NZ)), dma((4, NZ)),
-        dma((6,)), dma((6,)),
+        dma((9,)), dma((9,)),
         dma((PARTS, 16)), dma((PARTS, 16)),
         dma((NZ,)), dma((NZ,)),
         dma((12,)),
@@ -706,7 +732,7 @@
         out_shape=shapes,
         in_specs=[hbm] * 4,
         out_specs=(hbm,) * 4,
-        scratch_shapes=[pltpu.VMEM(shape.shape, shape.dtype) for shape in shapes] + [dma((2, 4))],
+        scratch_shapes=[pltpu.VMEM(shape.shape, shape.dtype) for shape in shapes] + [dma((2, 11))],
         compiler_params=pltpu.CompilerParams(vmem_limit_bytes=VMEM_BYTES),
         name="deliver",
     )(*outs)

time: 117 us -> 116 us (level)
  Pallas kernels: 115 us -> 113 us
    pallas_call x1, Pallas kernels: 112 us -> 111 us  [on_device(): pl.pallas_call(kernel, out_shape=shapes, in_specs=[pl.BlockSpec(memory_sp...]
where the time goes in v4:
time: 116 us; the launch traced here: 115 us
  Pallas kernels  113 us (97%)
  between operations  1.29 us (1%)
    pallas_call x1, Pallas kernels, on_device(): pl.pallas_call(kernel, out_shape=shapes, in_specs=[pl.BlockSpec(memory_sp...  111 us
    pallas_call x1, Pallas kernels, on_device(): pl.pallas_call(deliver, out_shape=shapes, in_specs=[hbm] * 4, out_specs=(...  2.52 us

profile of v4, /device:TPU:24, one launch (start us, length us, event | category | flops | bytes accessed | tf_op | source)
XLA Modules:
  0.0 114.7 jit_solution(632026135030000632)
XLA Ops:
  1.3 110.9 %attention_backward.1 = (bf16[8,4096]{1,0:T(8,128)(2,1)}, bf16[128,4096]{1,0:T(8,128)(2,1)}, bf16[128,4096]{1,0:T(8,128)(2,1)}, f32[64,512]{1,0:T(8,128)}) custom-call(bf16[8,4096]{1,0:T(8,128)(2,1)} %bitcast.11, bf16[8,4096]{1,0:T(8,128)(2,1)} %bitcast.12, bf16[8,4096]{1,0:T(8,128)(2,1)} %bitcast.13, bf16[128,4096]{1,0:T(8,128)(2,1)} %bitcast.9, ...), custom_call_target="tpu_custom_call" | custom-call | tf_op jit(solution)/shard_map/attention_backward/pallas_call | solution.py:716
  112.2 2.5 %deliver.1 = (bf16[8,4096]{1,0:T(8,128)(2,1)}, bf16[128,4096]{1,0:T(8,128)(2,1)}, bf16[128,4096]{1,0:T(8,128)(2,1)}, f32[64,512]{1,0:T(8,128)}) custom-call(bf16[8,4096]{1,0:T(8,128)(2,1)} %get-tuple-element.12.refs_0_, bf16[128,4096]{1,0:T(8,128)(2,1)} %get-tuple-element.13.refs_1_, bf16[128,4096]{1,0:T(8,128)(2,1)} %get-tuple-element.14.refs_2_, ...), custom_call_target="tpu_custom_call" | custom-call | tf_op jit(solution)/shard_map/deliver/pallas_call | solution.py:730
